TPU v7x, 512 devices: a whole 4x4x16 slice. The times are simulated.
512 devices in a mesh: ctx: 32 (over x, z_lo), dp: 16 (over y, z_hi, core).
Axes of the slice: x: 4, y: 4, z: 16 (z_hi: 2, z_lo: 8; z = z_hi * 8 + z_lo), core: 2. Of those that a mesh axis runs over, the one named last changes fastest.
Arguments:
- queries: bfloat16 [16, 4096, 2560], P('dp', 'ctx'), may hold values from -8 to 8
- keys: bfloat16 [16, 4096, 512], P('dp', 'ctx'), may hold values from -6 to 6
- values: bfloat16 [16, 4096, 512], P('dp', 'ctx'), may hold values from -6 to 6
- output_gradient: bfloat16 [16, 4096, 2560], P('dp', 'ctx'), may hold values from -6 to 6
- inputs: bfloat16 [16, 4096, 5120], P('dp', 'ctx'), may hold values from -6 to 6
- span_ids: int32 [64], P('ctx'), may hold values from 0 to 63, as said below
- segments: int32 [16, 4096], P('dp'), may hold values from 0 to 7, never falling along the last dimension, each value on 1 to 1024 neighbouring positions
Outputs:
- grad_queries: bfloat16 [16, 4096, 2560], P('dp', 'ctx')
- grad_wk: float32 [5120, 512], P('ctx')
- grad_wv: float32 [5120, 512], P('ctx')
Inputs may be any that keep to these rules, and one draw needn't show every extreme that they name: span_ids[2 r + 1] = 63 - span_ids[2 r] for every r, and each number appears once.
All inputs are finite; a program needn't handle non-finite values.
Results may differ from a plain program's by a relative error of at most 0.025.
Values may be sent and summed in bfloat16 or wider, within the bound.
No kernel may reach another device: no remote copies, remote signals or barrier semaphores. Data moves between devices by JAX's collectives and lax.ppermute only.
A program may use at most 64 MiB of HBM per device.

v0:
```python
import jax
import jax.numpy as jnp
from jax import lax
from jax.sharding import PartitionSpec as P

QUERY_HEADS = 20
KEY_VALUE_HEADS = 4
HEAD_SIZE = 128
WINDOW = 4


def shifted(block, axis, distance):
    devices = range(lax.axis_size(axis))
    route = [((i - distance) % len(devices), i) for i in devices]
    return lax.ppermute(block, axis, route)


def on_device(queries, keys, values, output_gradient, inputs, span_ids, segments):
    token_rows = queries.shape[1]
    half_rows = token_rows // 2
    sharing_queries = QUERY_HEADS // KEY_VALUE_HEADS
    score_scale = HEAD_SIZE ** (-0.5)
    row_index = jnp.arange(token_rows, dtype=jnp.int32)
    doc_ids = segments[0]

    def positions(span_pair):
        return (
            jnp.where(row_index < half_rows, span_pair[0], span_pair[1]) * half_rows
            + row_index % half_rows
        )

    pos_query = positions(span_ids)
    doc_query = doc_ids[pos_query]
    query_head_rows = queries[0].reshape(token_rows, KEY_VALUE_HEADS, sharing_queries, HEAD_SIZE)
    gradient_heads = output_gradient[0].reshape(
        token_rows, KEY_VALUE_HEADS, sharing_queries, HEAD_SIZE
    )
    own_tile = (keys[0], values[0], span_ids.astype(jnp.bfloat16))
    key_value_tiles = [own_tile]
    moving = own_tile
    for cycle_offset in range(1, WINDOW):
        moving = shifted((moving[0], moving[1], moving[2]), "ctx", 1)
        key_value_tiles.append(moving)
    key_collection = []
    value_list = []
    score_list = []
    mask_list = []
    for cycle_offset in range(WINDOW):
        key_block_tile = key_value_tiles[cycle_offset][0].reshape(
            token_rows, KEY_VALUE_HEADS, HEAD_SIZE
        )
        value_block_tile = key_value_tiles[cycle_offset][1].reshape(
            token_rows, KEY_VALUE_HEADS, HEAD_SIZE
        )
        pos_key = positions(key_value_tiles[cycle_offset][2].astype(jnp.int32))
        doc_key = doc_ids[pos_key]
        allowed = (pos_key[None, :] <= pos_query[:, None]) & (
            doc_key[None, :] == doc_query[:, None]
        )
        score_list.append(
            jnp.einsum(
                "tgcd,sgd->gcts",
                query_head_rows,
                key_block_tile,
                preferred_element_type=jnp.float32,
            )
            * score_scale
        )
        mask_list.append(allowed)
        key_collection.append(key_block_tile)
        value_list.append(value_block_tile)
    scores = jnp.concatenate(score_list, axis=-1)
    allowed_all = jnp.concatenate(mask_list, axis=-1)
    masked = jnp.where(allowed_all, scores, -1e30)
    peak = jnp.max(masked, axis=-1, keepdims=True)
    expd = jnp.where(allowed_all, jnp.exp(masked - peak), 0.0)
    probs = expd / jnp.sum(expd, axis=-1, keepdims=True)
    probs_b = probs.astype(jnp.bfloat16)
    output_sum = jnp.zeros((token_rows, KEY_VALUE_HEADS, sharing_queries, HEAD_SIZE), jnp.float32)
    for cycle_offset in range(WINDOW):
        block = probs_b[..., cycle_offset * token_rows : (cycle_offset + 1) * token_rows]
        output_sum = output_sum + jnp.einsum(
            "gcts,sgd->tgcd", block, value_list[cycle_offset], preferred_element_type=jnp.float32
        )
    out_b = output_sum.astype(jnp.bfloat16)
    delta = jnp.einsum(
        "tgc->gct", jnp.sum(gradient_heads.astype(jnp.float32) * out_b.astype(jnp.float32), axis=-1)
    )
    query_gradient_sum = jnp.zeros(
        (token_rows, KEY_VALUE_HEADS, sharing_queries, HEAD_SIZE), jnp.float32
    )
    contribs = []
    for cycle_offset in range(WINDOW):
        columns = slice(cycle_offset * token_rows, (cycle_offset + 1) * token_rows)
        dprobs = jnp.einsum(
            "tgcd,sgd->gcts",
            gradient_heads,
            value_list[cycle_offset],
            preferred_element_type=jnp.float32,
        )
        dscores = probs[..., columns] * (dprobs - delta[..., None])
        dscores_b = dscores.astype(jnp.bfloat16)
        query_gradient_sum = query_gradient_sum + jnp.einsum(
            "gcts,sgd->tgcd",
            dscores_b,
            key_collection[cycle_offset],
            preferred_element_type=jnp.float32,
        )
        key_gradient_term = (
            jnp.einsum(
                "gcts,tgcd->sgd", dscores_b, query_head_rows, preferred_element_type=jnp.float32
            )
            * score_scale
        )
        value_gradient_term = jnp.einsum(
            "gcts,tgcd->sgd",
            probs_b[..., columns],
            gradient_heads,
            preferred_element_type=jnp.float32,
        )
        contribs.append(
            (
                key_gradient_term.reshape(token_rows, KEY_VALUE_HEADS * HEAD_SIZE),
                value_gradient_term.reshape(token_rows, KEY_VALUE_HEADS * HEAD_SIZE),
            )
        )
    grad_queries = (
        (query_gradient_sum * score_scale)
        .astype(jnp.bfloat16)
        .reshape(1, token_rows, QUERY_HEADS * HEAD_SIZE)
    )
    total = contribs[WINDOW - 1]
    for cycle_offset in range(WINDOW - 1, 0, -1):
        total = shifted(total, "ctx", -1)
        total = (total[0] + contribs[cycle_offset - 1][0], total[1] + contribs[cycle_offset - 1][1])
    dkeys_b = total[0].astype(jnp.bfloat16)
    dvalues_b = total[1].astype(jnp.bfloat16)
    feature_cols = lax.all_to_all(inputs[0], "ctx", split_axis=1, concat_axis=0, tiled=True)
    dims = (((0,), (0,)), ((), ()))
    grad_wk, grad_wv = lax.psum(
        (
            lax.dot_general(
                feature_cols,
                lax.all_gather(dkeys_b, "ctx", axis=0, tiled=True),
                dims,
                preferred_element_type=jnp.float32,
            ),
            lax.dot_general(
                feature_cols,
                lax.all_gather(dvalues_b, "ctx", axis=0, tiled=True),
                dims,
                preferred_element_type=jnp.float32,
            ),
        ),
        "dp",
    )
    return (grad_queries, grad_wk, grad_wv)


def solution(mesh):
    return jax.shard_map(
        on_device,
        mesh=mesh,
        in_specs=(
            P("dp", "ctx", None),
            P("dp", "ctx", None),
            P("dp", "ctx", None),
            P("dp", "ctx", None),
            P("dp", "ctx", None),
            P("ctx"),
            P("dp", None),
        ),
        out_specs=(P("dp", "ctx", None), P("ctx", None), P("ctx", None)),
        check_vma=False,
    )
```

profile of v0, /device:TPU:1, one launch (start us, length us, event | category | flops | bytes accessed | tf_op | source)
XLA Modules:
  0.0 896.1 jit_solution(12627357301141958976)
XLA Ops:
  8.4 4.4 collective-permute-start.3
  13.4 3.5 collective-permute-start
  17.0 3.5 collective-permute-start.6
  32.3 2.5 multiply_add_fusion.2
  37.2 4.8 collective-permute-start.1
  42.0 8.2 collective-permute-done.1
  53.3 1.9 collective-permute-start.2
  55.2 11.1 %collective-permute-done.2 = bf16[2]{0:T(256)(128)(2,1)S(1)} collective-permute-done((bf16[2]{0:T(256)(128)(2,1)S(1)}, bf16[2]{0:T(256)(128)(2,1)S(1)}, u32[]{:S(2)}, u32[]{:S(2)}) %collective-permute-start.2) | collective-permute-done | bytes 36 | tf_op jit(solution)/shard_map/ppermute | solution.py:15
  66.9 2.5 multiply_add_fusion
  72.6 1.9 collective-permute-start.4
  74.5 1.5 fusion.6
  76.2 1.9 collective-permute-start.7
  78.1 9.0 collective-permute-done.4
  87.0 1.9 collective-permute-start.5
  89.0 1.4 fusion.5
  92.6 2.1 collective-permute-start.8
  94.7 6.8 collective-permute-done.5
  101.9 4.2 fusion.71
  106.0 3.4 fusion.65
  110.9 1.5 convolution_add_fusion.4
  112.6 2.0 fusion.30
  114.6 1.7 fusion.17
  116.3 1.7 fusion.18
  119.9 5.3 collective-permute-start.9
  125.6 2.9 collective-permute-done.9
  128.6 12.5 %collective-permute-start.10 = (f32[128,512]{0,1:T(8,128)S(1)}, f32[128,512]{0,1:T(8,128)S(1)}, u32[]{:S(2)}, u32[]{:S(2)}) collective-permute-start(f32[128,512]{0,1:T(8,128)S(1)} %bitcast_add_fusion.5), channel_id=1, source_target_pairs={{16,0},{32,16},{48,32},{64,48},{80,64},{96,80},{112,96},{128,112},... | collective-permute-start | bytes 786440 | tf_op jit(solution)/shard_map/ppermute | solution.py:15
  141.5 2.9 collective-permute-done.10
  144.4 12.5 %collective-permute-start.11 = (f32[128,512]{0,1:T(8,128)S(1)}, f32[128,512]{0,1:T(8,128)S(1)}, u32[]{:S(2)}, u32[]{:S(2)}) collective-permute-start(f32[128,512]{0,1:T(8,128)S(1)} %bitcast_add_fusion.4), channel_id=1, source_target_pairs={{16,0},{32,16},{48,32},{64,48},{80,64},{96,80},{112,96},{128,112},... | collective-permute-start | bytes 786440 | tf_op jit(solution)/shard_map/ppermute | solution.py:15
  157.4 2.9 collective-permute-done.11
  161.0 1.6 fusion.43
  162.7 12.5 %collective-permute-start.12 = (f32[128,512]{0,1:T(8,128)S(1)}, f32[128,512]{0,1:T(8,128)S(1)}, u32[]{:S(2)}, u32[]{:S(2)}) collective-permute-start(f32[128,512]{0,1:T(8,128)S(1)} %bitcast.301), channel_id=1, source_target_pairs={{16,0},{32,16},{48,32},{64,48},{80,64},{96,80},{112,96},{128,112},... | collective-permute-start | bytes 786440 | tf_op jit(solution)/shard_map/ppermute | solution.py:15
  175.2 1.5 fusion.46
  176.7 1.8 collective-permute-done.12
  178.5 12.7 %collective-permute-start.13 = (f32[128,512]{0,1:T(8,128)S(1)}, f32[128,512]{0,1:T(8,128)S(1)}, u32[]{:S(2)}, u32[]{:S(2)}) collective-permute-start(f32[128,512]{0,1:T(8,128)S(1)} %bitcast_add_fusion.2), channel_id=1, source_target_pairs={{16,0},{32,16},{48,32},{64,48},{80,64},{96,80},{112,96},{128,112},... | collective-permute-start | bytes 786440 | tf_op jit(solution)/shard_map/ppermute | solution.py:15
  191.6 2.8 collective-permute-done.13
  194.4 12.9 %collective-permute-start.14 = (f32[128,512]{0,1:T(8,128)S(1)}, f32[128,512]{0,1:T(8,128)S(1)}, u32[]{:S(2)}, u32[]{:S(2)}) collective-permute-start(f32[128,512]{0,1:T(8,128)S(1)} %bitcast_add_fusion.1), channel_id=1, source_target_pairs={{16,0},{32,16},{48,32},{64,48},{80,64},{96,80},{112,96},{128,112},... | collective-permute-start | bytes 786440 | tf_op jit(solution)/shard_map/ppermute | solution.py:15
  207.7 4.6 collective-permute-done.14
  213.0 2.4 copy.89
  215.4 12.5 %all-to-all-start = ((bf16[128,32,160]{0,2,1:T(8,128)(2,1)}), bf16[128,32,160]{0,2,1:T(8,128)(2,1)S(1)}, u32[]{:S(2)}, u32[]{:S(2)}) async-start(bf16[128,32,160]{0,2,1:T(8,128)(2,1)} %bitcast.76), calls=%async_computation | async-start | bytes 2621440 | tf_op jit(solution)/shard_map/all_to_all | solution.py:138
  227.9 1.4 fusion.72
  229.3 76.0 %all-to-all-done = bf16[128,32,160]{0,2,1:T(8,128)(2,1)S(1)} async-done(((bf16[128,32,160]{0,2,1:T(8,128)(2,1)}), bf16[128,32,160]{0,2,1:T(8,128)(2,1)S(1)}, u32[]{:S(2)}, u32[]{:S(2)}) %all-to-all-start) | async-done | bytes 1310752 | tf_op jit(solution)/shard_map/all_to_all | solution.py:138
  305.3 90.6 %all-gather.3.cloned.1.call-done = bf16[4096,512]{0,1:T(8,128)(2,1)} async-done(((bf16[128,512]{0,1:T(8,128)(2,1)}), bf16[4096,512]{0,1:T(8,128)(2,1)}) %all-gather.3.cloned.1.call-update) | async-done | bytes 4194320 | tf_op jit(solution)/shard_map/all_gather | solution.py:144
  395.9 4.5 fusion.31
  400.4 210.0 %all-gather.5.cloned.1.call-done = bf16[4096,512]{0,1:T(8,128)(2,1)} async-done(((bf16[128,512]{0,1:T(8,128)(2,1)}), bf16[4096,512]{0,1:T(8,128)(2,1)}) %all-gather.5.cloned.1.call-update) | async-done | bytes 4194320 | tf_op jit(solution)/shard_map/all_gather | solution.py:150
  610.4 4.9 fusion.34
  619.0 267.1 %all-reduce.3.cloned.1.call-done = (f32[160,512]{1,0:T(8,128)}, f32[160,512]{1,0:T(8,128)}) async-done(((f32[160,512]{1,0:T(8,128)}, f32[160,512]{1,0:T(8,128)}), (f32[160,512]{1,0:T(8,128)}, f32[160,512]{1,0:T(8,128)})) %all-reduce.3.cloned.1.call-update) | async-done | bytes 655376 | tf_op jit(solution)/shard_map/psum | solution.py:140
  886.1 1.7 copy.175
  887.8 1.7 copy.176
  (119 shorter events, 36.0 us)
Async XLA Ops:
  7.2 21.9 %copy-start = (s32[1,4096]{1,0:T(1,128)S(1)}, s32[1,4096]{1,0:T(1,128)}, u32[]{:S(2)}) copy-start(s32[1,4096]{1,0:T(1,128)} %param.13) | copy-start | bytes 49156
  7.2 19.8 %copy-start.14 = (bf16[1,128,2560]{2,1,0:T(8,128)(2,1)S(1)}, bf16[1,128,2560]{2,1,0:T(8,128)(2,1)}, u32[]{:S(2)}) copy-start(bf16[1,128,2560]{2,1,0:T(8,128)(2,1)} %param.10) | copy-start | bytes 1966084
  7.2 20.2 %copy-start.15 = (bf16[1,128,2560]{2,1,0:T(8,128)(2,1)S(1)}, bf16[1,128,2560]{2,1,0:T(8,128)(2,1)}, u32[]{:S(2)}) copy-start(bf16[1,128,2560]{2,1,0:T(8,128)(2,1)} %param.7) | copy-start | bytes 1966084
  7.2 388.7 %all-gather.3.cloned.1.call-start = ((), (), s32[]{:S(2)}) async-start(), calls=%async_computation.1 | async-start | bytes 4325376 | tf_op jit(solution)/shard_map/all_gather | solution.py:144
  8.4 64.3 %collective-permute-start.3 = (bf16[128,512]{0,1:T(8,128)(2,1)S(1)}, bf16[128,512]{0,1:T(8,128)(2,1)S(1)}, u32[]{:S(2)}, u32[]{:S(2)}) collective-permute-start(bf16[128,512]{0,1:T(8,128)(2,1)S(1)} %bitcast.303), channel_id=1, source_target_pairs={{496,0},{0,16},{16,32},{32,48},{48,64},{64,80},{80,96},{96,112},{1... | collective-permute-start | bytes 393224 | tf_op jit(solution)/shard_map/ppermute | solution.py:15
  13.4 18.3 %collective-permute-start = (bf16[2]{0:T(256)(128)(2,1)S(1)}, bf16[2]{0:T(256)(128)(2,1)S(1)}, u32[]{:S(2)}, u32[]{:S(2)}) collective-permute-start(bf16[2]{0:T(256)(128)(2,1)S(1)} %get-tuple-element.20), channel_id=1, source_target_pairs={{496,0},{0,16},{16,32},{32,48},{48,64},{64,80},{80,96},{96,112},{1... | collective-permute-start | bytes 20 | tf_op jit(solution)/shard_map/ppermute | solution.py:15
  17.0 59.1 %collective-permute-start.6 = (bf16[128,512]{1,0:T(8,128)(2,1)}, bf16[128,512]{1,0:T(8,128)(2,1)S(1)}, u32[]{:S(2)}, u32[]{:S(2)}) collective-permute-start(bf16[128,512]{1,0:T(8,128)(2,1)} %bitcast.302), channel_id=1, source_target_pairs={{496,0},{0,16},{16,32},{32,48},{48,64},{64,80},{80,96},{96,112},{1... | collective-permute-start | bytes 393224 | tf_op jit(solution)/shard_map/ppermute | solution.py:15
  37.2 13.0 %collective-permute-start.1 = (bf16[2]{0:T(256)(128)(2,1)S(1)}, bf16[2]{0:T(256)(128)(2,1)S(1)}, u32[]{:S(2)}, u32[]{:S(2)}) collective-permute-start(bf16[2]{0:T(256)(128)(2,1)S(1)} %collective-permute-done), channel_id=1, source_target_pairs={{496,0},{0,16},{16,32},{32,48},{48,64},{64,80},{80,96},{96,112},{1... | collective-permute-start | bytes 20 | tf_op jit(solution)/shard_map/ppermute | solution.py:15
  53.3 13.0 %collective-permute-start.2 = (bf16[2]{0:T(256)(128)(2,1)S(1)}, bf16[2]{0:T(256)(128)(2,1)S(1)}, u32[]{:S(2)}, u32[]{:S(2)}) collective-permute-start(bf16[2]{0:T(256)(128)(2,1)S(1)} %collective-permute-done.1), channel_id=1, source_target_pairs={{496,0},{0,16},{16,32},{32,48},{48,64},{64,80},{80,96},{96,112},{1... | collective-permute-start | bytes 20 | tf_op jit(solution)/shard_map/ppermute | solution.py:15
  72.6 17.8 %copy-start.16 = (bf16[128,512]{0,1:T(8,128)(2,1)}, bf16[128,512]{0,1:T(8,128)(2,1)S(1)}, u32[]{:S(2)}) copy-start(bf16[128,512]{0,1:T(8,128)(2,1)S(1)} %collective-permute-done.3) | copy-start | bytes 393220
  72.6 14.4 %collective-permute-start.4 = (bf16[128,512]{0,1:T(8,128)(2,1)S(1)}, bf16[128,512]{0,1:T(8,128)(2,1)S(1)}, u32[]{:S(2)}, u32[]{:S(2)}) collective-permute-start(bf16[128,512]{0,1:T(8,128)(2,1)S(1)} %collective-permute-done.3), channel_id=1, source_target_pairs={{496,0},{0,16},{16,32},{32,48},{48,64},{64,80},{80,96},{96,112},{1... | collective-permute-start | bytes 393224 | tf_op jit(solution)/shard_map/ppermute | solution.py:15
  76.2 15.4 %collective-permute-start.7 = (bf16[128,512]{1,0:T(8,128)(2,1)S(1)}, bf16[128,512]{1,0:T(8,128)(2,1)}, u32[]{:S(2)}, u32[]{:S(2)}) collective-permute-start(bf16[128,512]{1,0:T(8,128)(2,1)S(1)} %collective-permute-done.6), channel_id=1, source_target_pairs={{496,0},{0,16},{16,32},{32,48},{48,64},{64,80},{80,96},{96,112},{1... | collective-permute-start | bytes 393224 | tf_op jit(solution)/shard_map/ppermute | solution.py:15
  87.0 14.8 %copy-start.18 = (bf16[128,512]{0,1:T(8,128)(2,1)}, bf16[128,512]{0,1:T(8,128)(2,1)S(1)}, u32[]{:S(2)}) copy-start(bf16[128,512]{0,1:T(8,128)(2,1)S(1)} %collective-permute-done.4) | copy-start | bytes 393220
  87.0 14.4 %collective-permute-start.5 = (bf16[128,512]{0,1:T(8,128)(2,1)S(1)}, bf16[128,512]{0,1:T(8,128)(2,1)S(1)}, u32[]{:S(2)}, u32[]{:S(2)}) collective-permute-start(bf16[128,512]{0,1:T(8,128)(2,1)S(1)} %collective-permute-done.4), channel_id=1, source_target_pairs={{496,0},{0,16},{16,32},{32,48},{48,64},{64,80},{80,96},{96,112},{1... | collective-permute-start | bytes 393224 | tf_op jit(solution)/shard_map/ppermute | solution.py:15
  92.6 9.2 %copy-start.11 = (f32[4,5,128,128]{2,3,1,0:T(8,128)S(1)}, f32[4,5,128,128]{2,3,1,0:T(8,128)}, u32[]{:S(2)}) copy-start(f32[4,5,128,128]{2,3,1,0:T(8,128)} %fusion.6) | copy-start | bytes 3932164
  92.6 19.8 %collective-permute-start.8 = (bf16[128,512]{1,0:T(8,128)(2,1)}, bf16[128,512]{1,0:T(8,128)(2,1)S(1)}, u32[]{:S(2)}, u32[]{:S(2)}) collective-permute-start(bf16[128,512]{1,0:T(8,128)(2,1)} %collective-permute-done.7), channel_id=1, source_target_pairs={{496,0},{0,16},{16,32},{32,48},{48,64},{64,80},{80,96},{96,112},{1... | collective-permute-start | bytes 393224 | tf_op jit(solution)/shard_map/ppermute | solution.py:15
  101.5 4.6 copy-start.20
  109.4 1.5 copy-start.1
  110.9 7.1 slice-start
  112.5 2.0 copy-start.12
  112.6 5.5 slice-start.1
  118.1 23.1 %copy-start.7 = (bf16[4,5,128,128]{2,3,1,0:T(8,128)(2,1)}, bf16[4,5,128,128]{2,3,1,0:T(8,128)(2,1)S(1)}, u32[]{:S(2)}) copy-start(bf16[4,5,128,128]{2,3,1,0:T(8,128)(2,1)S(1)} %fusion.18) | copy-start | bytes 1966084
  118.1 1.0 copy-start.13
  119.1 6.1 copy-start.5
  119.5 6.1 copy-start.3
  119.9 8.6 collective-permute-start.9
  128.6 15.8 %collective-permute-start.10 = (f32[128,512]{0,1:T(8,128)S(1)}, f32[128,512]{0,1:T(8,128)S(1)}, u32[]{:S(2)}, u32[]{:S(2)}) collective-permute-start(f32[128,512]{0,1:T(8,128)S(1)} %bitcast_add_fusion.5), channel_id=1, source_target_pairs={{16,0},{32,16},{48,32},{64,48},{80,64},{96,80},{112,96},{128,112},... | collective-permute-start | bytes 786440 | tf_op jit(solution)/shard_map/ppermute | solution.py:15
  144.4 15.8 %collective-permute-start.11 = (f32[128,512]{0,1:T(8,128)S(1)}, f32[128,512]{0,1:T(8,128)S(1)}, u32[]{:S(2)}, u32[]{:S(2)}) collective-permute-start(f32[128,512]{0,1:T(8,128)S(1)} %bitcast_add_fusion.4), channel_id=1, source_target_pairs={{16,0},{32,16},{48,32},{64,48},{80,64},{96,80},{112,96},{128,112},... | collective-permute-start | bytes 786440 | tf_op jit(solution)/shard_map/ppermute | solution.py:15
  161.0 449.4 %all-gather.5.cloned.1.call-start = ((), (), s32[]{:S(2)}) async-start(), calls=%async_computation.2 | async-start | bytes 4325376 | tf_op jit(solution)/shard_map/all_gather | solution.py:150
  161.0 30.2 %copy-start.2 = (bf16[4,5,128,512]{2,3,1,0:T(8,128)(2,1)S(1)}, bf16[4,5,128,512]{2,3,1,0:T(8,128)(2,1)}, u32[]{:S(2)}) copy-start(bf16[4,5,128,512]{2,3,1,0:T(8,128)(2,1)} %copy-done.1) | copy-start | bytes 7864324
  162.7 15.8 %collective-permute-start.12 = (f32[128,512]{0,1:T(8,128)S(1)}, f32[128,512]{0,1:T(8,128)S(1)}, u32[]{:S(2)}, u32[]{:S(2)}) collective-permute-start(f32[128,512]{0,1:T(8,128)S(1)} %bitcast.301), channel_id=1, source_target_pairs={{16,0},{32,16},{48,32},{64,48},{80,64},{96,80},{112,96},{128,112},... | collective-permute-start | bytes 786440 | tf_op jit(solution)/shard_map/ppermute | solution.py:15
  178.5 15.9 %collective-permute-start.13 = (f32[128,512]{0,1:T(8,128)S(1)}, f32[128,512]{0,1:T(8,128)S(1)}, u32[]{:S(2)}, u32[]{:S(2)}) collective-permute-start(f32[128,512]{0,1:T(8,128)S(1)} %bitcast_add_fusion.2), channel_id=1, source_target_pairs={{16,0},{32,16},{48,32},{64,48},{80,64},{96,80},{112,96},{128,112},... | collective-permute-start | bytes 786440 | tf_op jit(solution)/shard_map/ppermute | solution.py:15
  194.4 17.9 %collective-permute-start.14 = (f32[128,512]{0,1:T(8,128)S(1)}, f32[128,512]{0,1:T(8,128)S(1)}, u32[]{:S(2)}, u32[]{:S(2)}) collective-permute-start(f32[128,512]{0,1:T(8,128)S(1)} %bitcast_add_fusion.1), channel_id=1, source_target_pairs={{16,0},{32,16},{48,32},{64,48},{80,64},{96,80},{112,96},{128,112},... | collective-permute-start | bytes 786440 | tf_op jit(solution)/shard_map/ppermute | solution.py:15
  215.4 89.9 %all-to-all-start = ((bf16[128,32,160]{0,2,1:T(8,128)(2,1)}), bf16[128,32,160]{0,2,1:T(8,128)(2,1)S(1)}, u32[]{:S(2)}, u32[]{:S(2)}) async-start(bf16[128,32,160]{0,2,1:T(8,128)(2,1)} %bitcast.76), calls=%async_computation | async-start | bytes 2621440 | tf_op jit(solution)/shard_map/all_to_all | solution.py:138
  227.9 658.2 %all-reduce.3.cloned.1.call-start = ((), (), s32[]{:S(2)}) async-start(), calls=%async_computation.3 | async-start | bytes 1310720 | tf_op jit(solution)/shard_map/psum | solution.py:140
  305.3 90.6 %copy-start.10 = (bf16[128,32,160]{0,2,1:T(8,128)(2,1)}, bf16[128,32,160]{0,2,1:T(8,128)(2,1)S(1)}, u32[]{:S(2)}) copy-start(bf16[128,32,160]{0,2,1:T(8,128)(2,1)S(1)} %all-to-all-done) | copy-start | bytes 3932164
  400.4 215.0 %copy-start.8 = (bf16[4,5,128,128]{2,3,1,0:T(8,128)(2,1)S(1)}, bf16[4,5,128,128]{2,3,1,0:T(8,128)(2,1)}, u32[]{:S(2)}) copy-start(bf16[4,5,128,128]{2,3,1,0:T(8,128)(2,1)} %copy-done.7) | copy-start | bytes 1966084
  400.4 215.0 %copy-start.17 = (bf16[128,512]{0,1:T(8,128)(2,1)S(1)}, bf16[128,512]{0,1:T(8,128)(2,1)}, u32[]{:S(2)}) copy-start(bf16[128,512]{0,1:T(8,128)(2,1)} %copy-done.16) | copy-start | bytes 393220
  610.4 5.0 copy-start.9
  615.4 1.1 copy-start.6
  615.4 1.1 copy-start.19
  616.5 1.1 copy-start.4
  616.5 1.1 copy-start.21
Sparse Core Ops, SparseCore 0:
  161.1 234.7 all-gather.2
  398.5 211.8 all-gather.4
  615.4 270.6 all-reduce.2
where the time goes:
time: 897 us; the launch traced here: 896 us
  waiting for transfers between devices  698 us (78%)
  starting transfers between devices  107 us (12%)
  matrix products  29.1 us (3%)
  local copies, waits for them, and re-layouts  24.6 us (3%)
  other arithmetic  23 us (3%)
  between operations  14.5 us (2%)
    psum x1, waiting for transfers between devices, on_device(): lax.psum((lax.dot_general(feature_cols, lax.all_gather(dkeys_b, 'ctx', ax...  267 us
    all_gather x1, waiting for transfers between devices, on_device(): lax.all_gather(dvalues_b, 'ctx', axis=0, tiled=True)  210 us
    ppermute x15, starting transfers between devices, shifted(): return lax.ppermute(block, axis, route)  94.4 us
    all_gather x1, waiting for transfers between devices, on_device(): lax.all_gather(dkeys_b, 'ctx', axis=0, tiled=True)  90.6 us
    all_to_all x1, waiting for transfers between devices, on_device(): lax.all_to_all(inputs[0], 'ctx', split_axis=1, concat_axis=0, tiled=True)  76 us
    ppermute x15, waiting for transfers between devices, shifted(): return lax.ppermute(block, axis, route)  54.1 us
  transfers between devices with their start and end apart: 19, of which 15 were waited for; matrix products, arithmetic and copies ran while one was open for 6% of the time, Pallas kernels for 0%

commit v1 on v0

v1 whole, which is shorter than its diff:
```python
import functools
import math

import jax
import jax.numpy as jnp
from jax import lax
from jax.experimental import pallas as pl
from jax.experimental.pallas import tpu as pltpu
from jax.sharding import Mesh, PartitionSpec as P

QUERY_HEADS = 20
KEY_VALUE_HEADS = 4
SHARING = QUERY_HEADS // KEY_VALUE_HEADS
HEAD = 128
ROWS = 128
HALF = ROWS // 2
WINDOW = 4
DOCUMENTS = 8
SCALE = HEAD ** (-0.5)
CTX = ("x", "zl")
DP = ("y", "zh", "c")
BF16 = jnp.bfloat16
F32 = jnp.float32


def shifted(block, distance):
    n = lax.axis_size(CTX)
    return lax.ppermute(block, CTX, [((i - distance) % n, i) for i in range(n)])


def exchange(blocks, axes):
    return lax.all_to_all(blocks, axes, 0, 0, tiled=True)


def dot(a, b, ca, cb):
    return lax.dot_general(a, b, (((ca,), (cb,)), ((), ())), preferred_element_type=F32)


def attention_kernel(
    span_ref, seg_ref, q_ref, g_ref, k_ref, v_ref, t1_ref, t2_ref, t3_ref,
    dq_ref, own_ref, r1_ref, r2_ref, r3_ref, bias_ref,
):
    tiles = (t1_ref, t2_ref, t3_ref)

    @pl.when(pl.program_id(0) == 0)
    def _():
        lane = lax.broadcasted_iota(jnp.int32, (1, ROWS), 1)
        pos_q = jnp.where(lane < HALF, span_ref[0] * HALF + lane, span_ref[1] * HALF + lane - HALF)
        seg = seg_ref[...]
        start = jnp.zeros((1, ROWS), jnp.int32)
        for doc in range(1, DOCUMENTS):
            first = jnp.sum((seg < doc).astype(F32), axis=1, keepdims=True).astype(jnp.int32)
            start = jnp.maximum(start, jnp.where(first <= pos_q, first, 0))
        row = lax.broadcasted_iota(jnp.int32, (HALF, ROWS), 0)
        for step in range(WINDOW):
            for half in range(2):
                if step == 0:
                    span = span_ref[half]
                else:
                    at = 2 * ROWS + 8 * half
                    span = tiles[step - 1][at : at + 8, :].astype(F32)[0:1, :].astype(jnp.int32)
                pos_k = span * HALF + row
                allowed = (pos_k <= pos_q) & (pos_k >= start)
                at = step * ROWS + half * HALF
                bias_ref[at : at + HALF, :] = jnp.where(allowed, 0.0, -1e30)

    k = jnp.concatenate([k_ref[...]] + [t[0:ROWS, :] for t in tiles], axis=0)
    v = jnp.concatenate([v_ref[...]] + [t[ROWS : 2 * ROWS, :] for t in tiles], axis=0)
    heads = [slice(c * HEAD, (c + 1) * HEAD) for c in range(SHARING)]
    q = jnp.concatenate([q_ref[:, h] for h in heads], axis=0)
    g = jnp.concatenate([g_ref[:, h] for h in heads], axis=0)
    bias = bias_ref[...]
    s = dot(k, q, 1, 1) + jnp.concatenate([bias] * SHARING, axis=1)
    e = jnp.exp2((s - jnp.max(s, axis=0, keepdims=True)) * (SCALE * math.log2(math.e)))
    p = e * (1.0 / jnp.sum(e, axis=0, keepdims=True))
    dp = dot(v, g, 1, 1)
    delta = jnp.sum(p * dp, axis=0, keepdims=True)
    ds = (p * (dp - delta)).astype(BF16)
    dv = dot(p.astype(BF16), g, 1, 0)
    dk = dot(ds, q, 1, 0) * SCALE
    dq = (dot(ds, k, 0, 0) * SCALE).astype(BF16)
    for c, h in enumerate(heads):
        dq_ref[:, h] = dq[c * ROWS : (c + 1) * ROWS, :]
    own_ref[0] = dk[0:ROWS]
    own_ref[1] = dv[0:ROWS]
    for step, ref in enumerate((r1_ref, r2_ref, r3_ref), 1):
        rows = slice(step * ROWS, (step + 1) * ROWS)
        ref[0] = dk[rows].astype(BF16)
        ref[1] = dv[rows].astype(BF16)


def attention(span, segments, queries, gradient, keys, values, tiles):
    wide = pl.BlockSpec((None, ROWS, SHARING * HEAD), lambda i: (0, 0, i))
    narrow = pl.BlockSpec((None, ROWS, HEAD), lambda i: (0, 0, i))
    tile = pl.BlockSpec((tiles[0].shape[0], HEAD), lambda i: (0, i))
    term = pl.BlockSpec((2, None, ROWS, HEAD), lambda i: (0, i // 2, 0, i % 2))
    terms = (2, 2, ROWS, 2 * HEAD)
    work = QUERY_HEADS * ROWS * WINDOW * ROWS
    return pl.pallas_call(
        attention_kernel,
        grid=(KEY_VALUE_HEADS,),
        in_specs=[
            pl.BlockSpec(memory_space=pltpu.SMEM),
            pl.BlockSpec(segments.shape, lambda i: (0, 0)),
            wide, wide, narrow, narrow, tile, tile, tile,
        ],
        out_specs=[wide, term, term, term, term],
        out_shape=[
            jax.ShapeDtypeStruct(queries.shape, BF16),
            jax.ShapeDtypeStruct(terms, F32),
            jax.ShapeDtypeStruct(terms, BF16),
            jax.ShapeDtypeStruct(terms, BF16),
            jax.ShapeDtypeStruct(terms, BF16),
        ],
        scratch_shapes=[pltpu.VMEM((WINDOW * ROWS, ROWS), F32)],
        compiler_params=pltpu.CompilerParams(vmem_limit_bytes=48 * 1024 * 1024),
        cost_estimate=pl.CostEstimate(
            flops=10 * HEAD * work, bytes_accessed=5 * 1024 * 1024, transcendentals=work
        ),
        name="attention",
    )(span, segments, queries, gradient, keys, values, *tiles)


def on_device(queries, keys, values, output_gradient, inputs, span_ids, segments):
    nx, ny, nzl, nzh, nc = (lax.axis_size(a) for a in ("x", "y", "zl", "zh", "c"))
    rows, features = inputs.shape[1:]
    part = features // nx
    with jax.named_scope("inputs_exchange"):
        by_x = inputs[0].reshape(rows, nx, part).transpose(1, 0, 2)
        blocks = jnp.broadcast_to(by_x[:, None], (nx, ny, rows, part)).reshape(nx * ny, rows, part)
        features_x = exchange(blocks, ("x", "y")).reshape(nx * ny * rows, part)
    with jax.named_scope("keys_values_halo"):
        numbers = jnp.broadcast_to(
            jnp.repeat(span_ids, 8, total_repeat_length=16)[:, None], (16, keys.shape[2])
        )
        tile = jnp.concatenate([keys[0], values[0], numbers.astype(BF16)], axis=0)
        tiles = [shifted(tile, step) for step in range(1, WINDOW)]
    with jax.named_scope("attention"):
        grad_queries, own, *terms = attention(
            span_ids, segments, queries, output_gradient, keys, values, tiles
        )
    with jax.named_scope("gradient_return"):
        back = [shifted(term, -step) for step, term in enumerate(terms, 1)]
        total = (own + sum(b.astype(F32) for b in back)).astype(BF16)
    with jax.named_scope("gradient_exchange"):
        by_y = total.reshape(ny, rows, 2 * HEAD)
        blocks = jnp.broadcast_to(by_y[None], (nx, ny, rows, 2 * HEAD))
        columns = exchange(blocks.reshape(nx * ny, rows, 2 * HEAD), ("x", "y"))
        columns = columns.reshape(nx * ny * rows, 2 * HEAD)
    with jax.named_scope("projection"):
        partial = dot(features_x, columns, 0, 0)
    with jax.named_scope("core_sum"):
        halves = partial.astype(BF16).reshape(part, nc, HEAD).transpose(1, 0, 2)
        pair = jnp.sum(exchange(halves, ("c",)).astype(F32), axis=0)
    with jax.named_scope("z_sum"):
        piece = part // (nzl * nzh)
        pieces = exchange(pair.astype(BF16).reshape(nzl * nzh, piece, HEAD), ("zl", "zh"))
        summed = jnp.sum(pieces.astype(F32), axis=0).astype(BF16)
    with jax.named_scope("replicate"):
        every = exchange(jnp.broadcast_to(summed[None], (ny * nzh * nc, piece, HEAD)), DP)
        every = every.reshape(ny, nzh, nc, piece, HEAD).transpose(1, 3, 0, 2, 4)
        every = every.reshape(nzh * piece, 2, ny * nc * HEAD // 2).astype(F32)
    return grad_queries, every[:, 0], every[:, 1]


def solution(mesh):
    axes = Mesh(mesh.devices.reshape(4, 8, 4, 2, 2), CTX + DP)
    by_row = P(DP, CTX, None)
    return jax.shard_map(
        on_device,
        mesh=axes,
        in_specs=(by_row, by_row, by_row, by_row, by_row, P(CTX), P(DP, None)),
        out_specs=(by_row, P(CTX, None), P(CTX, None)),
        check_vma=False,
    )
```

time: 897 us -> 271 us (0.30)
  the two profiles are of different devices: /device:TPU:1 before, /device:TPU:8 now
where the time goes in v1:
time: 271 us
  blocking collectives  142 us (52%)
  waiting for transfers between devices  66.7 us (25%)
  starting transfers between devices  34.4 us (13%)
  local copies, waits for them, and re-layouts  12.4 us (5%)
  Pallas kernels  7.89 us (3%)
  other arithmetic  3.41 us (1%)
  matrix products  2.8 us (1%)
    all_to_all x4, blocking collectives, exchange(): return lax.all_to_all(blocks, axes, 0, 0, tiled=True)  142 us
    ppermute x6, waiting for transfers between devices, shifted(): return lax.ppermute(block, CTX, [((i - distance) % n, i) for i in range(n)])  52.1 us
    ppermute x6, starting transfers between devices, shifted(): return lax.ppermute(block, CTX, [((i - distance) % n, i) for i in range(n)])  28.4 us
    all_to_all x1, waiting for transfers between devices, exchange(): return lax.all_to_all(blocks, axes, 0, 0, tiled=True)  14.5 us
    pallas_call x1, Pallas kernels, attention(): pl.pallas_call(attention_kernel, grid=(KEY_VALUE_HEADS,), in_specs=[pl.Bl...  7.89 us
    unnamed x15, local copies, waits for them, and re-layouts  6.23 us
    all_to_all x1, starting transfers between devices, exchange(): return lax.all_to_all(blocks, axes, 0, 0, tiled=True)  5.97 us
  transfers between devices with their start and end apart: 7, of which 4 were waited for; matrix products, arithmetic and copies ran while one was open for 0% of the time, Pallas kernels for 0%

profile of v1, /device:TPU:8, one launch (start us, length us, event | category | flops | bytes accessed | tf_op | source)
XLA Modules:
  0.0 270.5 jit_solution(2645316290612700851)
XLA Ops:
  0.6 1.3 fusion.2
  1.9 2.0 select_convert_fusion
  3.9 1.1 maximum_maximum_fusion
  5.0 6.5 %collective-permute-start.2 = (bf16[272,512]{1,0:T(8,128)(2,1)S(1)}, bf16[272,512]{1,0:T(8,128)(2,1)S(1)}, u32[]{:S(2)}, u32[]{:S(2)}) collective-permute-start(bf16[272,512]{1,0:T(8,128)(2,1)S(1)} %maximum_maximum_fusion), channel_id=1, source_target_pairs={{464,0},{480,16},{496,32},{0,48},{16,64},{32,80},{48,96},{64,112},... | collective-permute-start | bytes 835592 | tf_op jit(solution)/shard_map/keys_values_halo/ppermute | solution.py:28
  11.5 6.4 %collective-permute-start.1 = (bf16[272,512]{1,0:T(8,128)(2,1)S(1)}, bf16[272,512]{1,0:T(8,128)(2,1)S(1)}, u32[]{:S(2)}, u32[]{:S(2)}) collective-permute-start(bf16[272,512]{1,0:T(8,128)(2,1)S(1)} %maximum_maximum_fusion), channel_id=1, source_target_pairs={{480,0},{496,16},{0,32},{16,48},{32,64},{48,80},{64,96},{80,112},{... | collective-permute-start | bytes 835592 | tf_op jit(solution)/shard_map/keys_values_halo/ppermute | solution.py:28
  17.9 3.8 %collective-permute-start = (bf16[272,512]{1,0:T(8,128)(2,1)S(1)}, bf16[272,512]{1,0:T(8,128)(2,1)S(1)}, u32[]{:S(2)}, u32[]{:S(2)}) collective-permute-start(bf16[272,512]{1,0:T(8,128)(2,1)S(1)} %maximum_maximum_fusion), channel_id=1, source_target_pairs={{496,0},{0,16},{16,32},{32,48},{48,64},{64,80},{80,96},{96,112},{1... | collective-permute-start | bytes 835592 | tf_op jit(solution)/shard_map/keys_values_halo/ppermute | solution.py:28
  21.8 32.4 %collective-permute-done.2.t3_ref = bf16[272,512]{1,0:T(8,128)(2,1)S(1)} collective-permute-done((bf16[272,512]{1,0:T(8,128)(2,1)S(1)}, bf16[272,512]{1,0:T(8,128)(2,1)S(1)}, u32[]{:S(2)}, u32[]{:S(2)}) %collective-permute-start.2) | collective-permute-done | bytes 278560 | tf_op jit(solution)/shard_map/keys_values_halo/ppermute | solution.py:28
  54.1 0.0 collective-permute-done.1.t2_ref
  54.1 0.0 collective-permute-done.t1_ref
  54.1 0.0 copy-start
  54.1 0.9 copy-done
  55.0 0.0 copy-start.1
  55.0 0.9 copy-done.1
  55.9 0.0 copy-start.2
  55.9 0.7 copy-done.2
  56.6 0.0 copy-start.3
  56.6 1.1 copy-done.3
  57.7 0.0 copy-start.4
  57.7 1.1 copy-done.4
  58.8 0.7 copy-done.5
  59.5 7.9 %attention.1 = (bf16[1,128,2560]{2,1,0:T(8,128)(2,1)}, f32[2,2,128,256]{3,2,1,0:T(8,128)S(1)}, bf16[2,2,128,256]{3,2,1,0:T(8,128)(2,1)S(1)}, bf16[2,2,128,256]{3...) custom-call(s32[2]{0:T(128)S(1)} %copy-done.2, s32[1,4096]{1,0:T(1,128)S(1)} %copy-done.5, ...), custom_call_target="tpu_custom_call" | custom-call | flops 1677721600 | bytes 5242880 | tf_op jit(solution)/shard_map/attention/attention/pallas_call | solution.py:99
  67.4 1.9 collective-permute-start.3
  69.3 7.8 %collective-permute-start.4 = (bf16[2,2,128,256]{3,2,1,0:T(8,128)(2,1)S(1)}, bf16[2,2,128,256]{3,2,1,0:T(8,128)(2,1)S(1)}, u32[]{:S(2)}, u32[]{:S(2)}) collective-permute-start(bf16[2,2,128,256]{3,2,1,0:T(8,128)(2,1)S(1)} %get-tuple-element.23), channel_id=1, source_target_pairs={{32,0},{48,16},{64,32},{80,48},{96,64},{112,80},{128,96},{144,112}... | collective-permute-start | bytes 786440 | tf_op jit(solution)/shard_map/gradient_return/ppermute | solution.py:28
  77.2 1.9 collective-permute-start.5
  79.1 0.0 collective-permute-done.3
  79.1 6.5 %collective-permute-done.4 = bf16[2,2,128,256]{3,2,1,0:T(8,128)(2,1)S(1)} collective-permute-done((bf16[2,2,128,256]{3,2,1,0:T(8,128)(2,1)S(1)}, bf16[2,2,128,256]{3,2,1,0:T(8,128)(2,1)S(1)}, u32[]{:S(2)}, u32[]{:S(2)}) %collective-permute-start.4) | collective-permute-done | bytes 262176 | tf_op jit(solution)/shard_map/gradient_return/ppermute | solution.py:28
  85.6 13.3 %collective-permute-done.5 = bf16[2,2,128,256]{3,2,1,0:T(8,128)(2,1)S(1)} collective-permute-done((bf16[2,2,128,256]{3,2,1,0:T(8,128)(2,1)S(1)}, bf16[2,2,128,256]{3,2,1,0:T(8,128)(2,1)S(1)}, u32[]{:S(2)}, u32[]{:S(2)}) %collective-permute-start.5) | collective-permute-done | bytes 262176 | tf_op jit(solution)/shard_map/gradient_return/ppermute | solution.py:28
  98.9 0.1 add_convert_fusion
  99.0 0.2 copy.20
  99.2 1.2 broadcast_in_dim.14
  100.4 6.0 %all-to-all-start = ((bf16[16,128,256]{1,2,0:T(8,128)(2,1)}), bf16[16,128,256]{1,2,0:T(8,128)(2,1)}, u32[]{:S(2)}, u32[]{:S(2)}) async-start(bf16[16,128,256]{1,2,0:T(8,128)(2,1)} %bitcast.5), calls=%async_computation | async-start | bytes 2097152 | tf_op jit(solution)/shard_map/gradient_exchange/all_to_all | solution.py:32
  106.4 0.0 copy-done.6
  106.4 1.0 squeeze.17
  107.4 0.1 copy.21
  107.5 14.5 %all-to-all-done = bf16[16,128,256]{1,2,0:T(8,128)(2,1)} async-done(((bf16[16,128,256]{1,2,0:T(8,128)(2,1)}), bf16[16,128,256]{1,2,0:T(8,128)(2,1)}, u32[]{:S(2)}, u32[]{:S(2)}) %all-to-all-start) | async-done | bytes 1048608 | tf_op jit(solution)/shard_map/gradient_exchange/all_to_all | solution.py:32
  122.1 0.5 broadcast_in_dim.15
  122.6 63.5 %all_to_all.25 = bf16[16,128,1280]{2,1,0:T(8,128)(2,1)S(1)} all-to-all(bf16[16,128,1280]{2,1,0:T(8,128)(2,1)S(1)} %bitcast.30), channel_id=1, replica_groups=mesh['x'=4,'zl'=8,'y'=4,'zh'=2,'c'=2] {'x','y'}, dimensions={0} | all-to-all | bytes 10485760 | tf_op jit(solution)/shard_map/inputs_exchange/all_to_all | solution.py:32
  186.1 2.8 %fusion = bf16[256,1280]{1,0:T(8,128)(2,1)S(1)} fusion(bf16[16,128,256]{1,2,0:T(8,128)(2,1)} %all-to-all-done, bf16[16,128,1280]{2,1,0:T(8,128)(2,1)S(1)} %all_to_all.25), kind=kOutput, calls=%fused_computation.1 | convolution fusion | flops 1342504960 | bytes 6946816 | tf_op jit(solution)/shard_map/projection/dot_general | solution.py:36
  188.9 4.3 %all_to_all.26 = bf16[2,1280,128]{1,2,0:T(8,128)(2,1)S(1)} all-to-all(bf16[2,1280,128]{1,2,0:T(8,128)(2,1)S(1)} %bitcast.35), channel_id=1, replica_groups=mesh['x'=4,'zl'=8,'y'=4,'zh'=2,'c'=2] {'c'}, dimensions={0} | all-to-all | bytes 1310720 | tf_op jit(solution)/shard_map/core_sum/all_to_all | solution.py:32
  193.2 0.1 reduce_sum.24
  193.3 0.2 copy.22
  193.5 42.2 %all_to_all.27 = bf16[16,80,128]{2,1,0:T(8,128)(2,1)S(1)} all-to-all(bf16[16,80,128]{2,1,0:T(8,128)(2,1)S(1)} %bitcast.32), channel_id=1, replica_groups=mesh['x'=4,'zl'=8,'y'=4,'zh'=2,'c'=2] {'zl','zh'}, dimensions={0} | all-to-all | bytes 655360 | tf_op jit(solution)/shard_map/z_sum/all_to_all | solution.py:32
  235.7 0.1 reduce_sum.25
  235.8 32.1 %all_to_all.28 = bf16[16,80,128]{2,1,0:T(8,128)(2,1)S(1)} all-to-all(bf16[16,80,128]{2,1,0:T(8,128)(2,1)S(1)} %broadcast_in_dim.16), channel_id=1, replica_groups=mesh['x'=4,'zl'=8,'y'=4,'zh'=2,'c'=2] {'y','zh','c'}, dimensions={0} | all-to-all | bytes 655360 | tf_op jit(solution)/shard_map/replicate/all_to_all | solution.py:32
  268.0 0.3 copy.23
  268.4 0.8 reshape.71
  269.1 0.5 fusion.1
  269.6 0.9 copy_bitcast_fusion
  (5 shorter events, 0.1 us)
Async XLA Ops:
  5.0 49.1 %collective-permute-start.2 = (bf16[272,512]{1,0:T(8,128)(2,1)S(1)}, bf16[272,512]{1,0:T(8,128)(2,1)S(1)}, u32[]{:S(2)}, u32[]{:S(2)}) collective-permute-start(bf16[272,512]{1,0:T(8,128)(2,1)S(1)} %maximum_maximum_fusion), channel_id=1, source_target_pairs={{464,0},{480,16},{496,32},{0,48},{16,64},{32,80},{48,96},{64,112},... | collective-permute-start | bytes 835592 | tf_op jit(solution)/shard_map/keys_values_halo/ppermute | solution.py:28
  11.5 42.6 %collective-permute-start.1 = (bf16[272,512]{1,0:T(8,128)(2,1)S(1)}, bf16[272,512]{1,0:T(8,128)(2,1)S(1)}, u32[]{:S(2)}, u32[]{:S(2)}) collective-permute-start(bf16[272,512]{1,0:T(8,128)(2,1)S(1)} %maximum_maximum_fusion), channel_id=1, source_target_pairs={{480,0},{496,16},{0,32},{16,48},{32,64},{48,80},{64,96},{80,112},{... | collective-permute-start | bytes 835592 | tf_op jit(solution)/shard_map/keys_values_halo/ppermute | solution.py:28
  17.9 36.2 %collective-permute-start = (bf16[272,512]{1,0:T(8,128)(2,1)S(1)}, bf16[272,512]{1,0:T(8,128)(2,1)S(1)}, u32[]{:S(2)}, u32[]{:S(2)}) collective-permute-start(bf16[272,512]{1,0:T(8,128)(2,1)S(1)} %maximum_maximum_fusion), channel_id=1, source_target_pairs={{496,0},{0,16},{16,32},{32,48},{48,64},{64,80},{80,96},{96,112},{1... | collective-permute-start | bytes 835592 | tf_op jit(solution)/shard_map/keys_values_halo/ppermute | solution.py:28
  54.1 0.9 copy-start
  55.0 0.9 copy-start.1
  55.9 0.7 copy-start.2
  56.6 1.1 copy-start.3
  57.7 1.1 copy-start.4
  58.8 0.7 copy-start.5
  59.5 46.9 %copy-start.6 = (bf16[1,128,5120]{2,1,0:T(8,128)(2,1)S(1)}, bf16[1,128,5120]{2,1,0:T(8,128)(2,1)}, u32[]{:S(2)}) copy-start(bf16[1,128,5120]{2,1,0:T(8,128)(2,1)} %param.13) | copy-start | bytes 3932164
  67.4 11.7 %collective-permute-start.3 = (bf16[2,2,128,256]{3,2,1,0:T(8,128)(2,1)S(1)}, bf16[2,2,128,256]{3,2,1,0:T(8,128)(2,1)S(1)}, u32[]{:S(2)}, u32[]{:S(2)}) collective-permute-start(bf16[2,2,128,256]{3,2,1,0:T(8,128)(2,1)S(1)} %get-tuple-element.22), channel_id=1, source_target_pairs={{16,0},{32,16},{48,32},{64,48},{80,64},{96,80},{112,96},{128,112},... | collective-permute-start | bytes 786440 | tf_op jit(solution)/shard_map/gradient_return/ppermute | solution.py:28
  69.3 16.3 %collective-permute-start.4 = (bf16[2,2,128,256]{3,2,1,0:T(8,128)(2,1)S(1)}, bf16[2,2,128,256]{3,2,1,0:T(8,128)(2,1)S(1)}, u32[]{:S(2)}, u32[]{:S(2)}) collective-permute-start(bf16[2,2,128,256]{3,2,1,0:T(8,128)(2,1)S(1)} %get-tuple-element.23), channel_id=1, source_target_pairs={{32,0},{48,16},{64,32},{80,48},{96,64},{112,80},{128,96},{144,112}... | collective-permute-start | bytes 786440 | tf_op jit(solution)/shard_map/gradient_return/ppermute | solution.py:28
  77.2 21.7 %collective-permute-start.5 = (bf16[2,2,128,256]{3,2,1,0:T(8,128)(2,1)S(1)}, bf16[2,2,128,256]{3,2,1,0:T(8,128)(2,1)S(1)}, u32[]{:S(2)}, u32[]{:S(2)}) collective-permute-start(bf16[2,2,128,256]{3,2,1,0:T(8,128)(2,1)S(1)} %get-tuple-element.24), channel_id=1, source_target_pairs={{48,0},{64,16},{80,32},{96,48},{112,64},{128,80},{144,96},{160,112... | collective-permute-start | bytes 786440 | tf_op jit(solution)/shard_map/gradient_return/ppermute | solution.py:28
  100.4 21.7 %all-to-all-start = ((bf16[16,128,256]{1,2,0:T(8,128)(2,1)}), bf16[16,128,256]{1,2,0:T(8,128)(2,1)}, u32[]{:S(2)}, u32[]{:S(2)}) async-start(bf16[16,128,256]{1,2,0:T(8,128)(2,1)} %bitcast.5), calls=%async_computation | async-start | bytes 2097152 | tf_op jit(solution)/shard_map/gradient_exchange/all_to_all | solution.py:32

commit v2 on v1

--- a/solution.py
+++ b/solution.py
@@ -20,6 +20,7 @@
 CTX = ("x", "zl")
 DP = ("y", "zh", "c")
 BF16 = jnp.bfloat16
+VMEM_LIMIT = 60 * 1024 * 1024
 F32 = jnp.float32
 
 
@@ -89,6 +90,26 @@
         ref[1] = dv[rows].astype(BF16)
 
 
+def sum_kernel(own_ref, b1_ref, b2_ref, b3_ref, after_ref, out_ref):
+    del after_ref
+    total = own_ref[...]
+    for ref in (b1_ref, b2_ref, b3_ref):
+        total = total + ref[...].astype(F32)
+    out_ref[...] = total.astype(BF16)
+
+
+def sum_terms(own, back, after):
+    whole = pl.BlockSpec(memory_space=pltpu.VMEM)
+    return pl.pallas_call(
+        sum_kernel,
+        in_specs=[whole] * 4 + [pl.BlockSpec(memory_space=pl.ANY)],
+        out_specs=whole,
+        out_shape=jax.ShapeDtypeStruct(own.shape, BF16),
+        cost_estimate=pl.CostEstimate(flops=own.size * 4, bytes_accessed=own.size * 18, transcendentals=0),
+        name="sum_terms",
+    )(own, *back, after)
+
+
 def attention(span, segments, queries, gradient, keys, values, tiles):
     wide = pl.BlockSpec((None, ROWS, SHARING * HEAD), lambda i: (0, 0, i))
     narrow = pl.BlockSpec((None, ROWS, HEAD), lambda i: (0, 0, i))
@@ -113,7 +134,7 @@
             jax.ShapeDtypeStruct(terms, BF16),
         ],
         scratch_shapes=[pltpu.VMEM((WINDOW * ROWS, ROWS), F32)],
-        compiler_params=pltpu.CompilerParams(vmem_limit_bytes=48 * 1024 * 1024),
+        compiler_params=pltpu.CompilerParams(vmem_limit_bytes=VMEM_LIMIT),
         cost_estimate=pl.CostEstimate(
             flops=10 * HEAD * work, bytes_accessed=5 * 1024 * 1024, transcendentals=work
         ),
@@ -125,26 +146,23 @@
     nx, ny, nzl, nzh, nc = (lax.axis_size(a) for a in ("x", "y", "zl", "zh", "c"))
     rows, features = inputs.shape[1:]
     part = features // nx
+    with jax.named_scope("keys_values_halo"):
+        numbers = jnp.broadcast_to(span_ids.astype(BF16)[:, None, None], (2, 8, keys.shape[2]))
+        tile = jnp.concatenate([keys[0], values[0], numbers.reshape(16, keys.shape[2])], axis=0)
+        tiles = [shifted(tile, step) for step in range(1, WINDOW)]
     with jax.named_scope("inputs_exchange"):
         by_x = inputs[0].reshape(rows, nx, part).transpose(1, 0, 2)
         blocks = jnp.broadcast_to(by_x[:, None], (nx, ny, rows, part)).reshape(nx * ny, rows, part)
         features_x = exchange(blocks, ("x", "y")).reshape(nx * ny * rows, part)
-    with jax.named_scope("keys_values_halo"):
-        numbers = jnp.broadcast_to(
-            jnp.repeat(span_ids, 8, total_repeat_length=16)[:, None], (16, keys.shape[2])
-        )
-        tile = jnp.concatenate([keys[0], values[0], numbers.astype(BF16)], axis=0)
-        tiles = [shifted(tile, step) for step in range(1, WINDOW)]
     with jax.named_scope("attention"):
         grad_queries, own, *terms = attention(
             span_ids, segments, queries, output_gradient, keys, values, tiles
         )
     with jax.named_scope("gradient_return"):
         back = [shifted(term, -step) for step, term in enumerate(terms, 1)]
-        total = (own + sum(b.astype(F32) for b in back)).astype(BF16)
+        blocks = sum_terms(own, back, features_x)
     with jax.named_scope("gradient_exchange"):
-        by_y = total.reshape(ny, rows, 2 * HEAD)
-        blocks = jnp.broadcast_to(by_y[None], (nx, ny, rows, 2 * HEAD))
+        blocks = jnp.broadcast_to(blocks.reshape(ny, rows, 2 * HEAD)[None], (nx, ny, rows, 2 * HEAD))
         columns = exchange(blocks.reshape(nx * ny, rows, 2 * HEAD), ("x", "y"))
         columns = columns.reshape(nx * ny * rows, 2 * HEAD)
     with jax.named_scope("projection"):
@@ -153,14 +171,16 @@
         halves = partial.astype(BF16).reshape(part, nc, HEAD).transpose(1, 0, 2)
         pair = jnp.sum(exchange(halves, ("c",)).astype(F32), axis=0)
     with jax.named_scope("z_sum"):
-        piece = part // (nzl * nzh)
-        pieces = exchange(pair.astype(BF16).reshape(nzl * nzh, piece, HEAD), ("zl", "zh"))
+        piece = part // nzl
+        pieces = exchange(pair.astype(BF16).reshape(nzl, piece, HEAD), ("zl",))
         summed = jnp.sum(pieces.astype(F32), axis=0).astype(BF16)
+        other = lax.ppermute(summed, ("zh",), [(i, 1 - i) for i in range(nzh)])
+        summed = (summed.astype(F32) + other.astype(F32)).astype(BF16)
     with jax.named_scope("replicate"):
-        every = exchange(jnp.broadcast_to(summed[None], (ny * nzh * nc, piece, HEAD)), DP)
-        every = every.reshape(ny, nzh, nc, piece, HEAD).transpose(1, 3, 0, 2, 4)
-        every = every.reshape(nzh * piece, 2, ny * nc * HEAD // 2).astype(F32)
-    return grad_queries, every[:, 0], every[:, 1]
+        every = exchange(jnp.broadcast_to(summed[None], (ny * nc, piece, HEAD)), ("y", "c"))
+        every = every.reshape(2, ny * nc // 2, piece, HEAD).transpose(0, 2, 1, 3).astype(F32)
+        every = every.reshape(2, piece, ny * nc * HEAD // 2)
+    return grad_queries, every[0], every[1]
 
 
 def solution(mesh):

time: 271 us -> 205 us (0.76)
  the two profiles are of different devices: /device:TPU:8 before, /device:TPU:1 now
where the time goes in v2:
time: 205 us
  blocking collectives  74.4 us (36%)
  waiting for transfers between devices  54.2 us (26%)
  starting transfers between devices  49.2 us (24%)
  local copies, waits for them, and re-layouts  11.1 us (5%)
  Pallas kernels  10.4 us (5%)
  matrix products  4.07 us (2%)
    all_to_all x4, blocking collectives, exchange(): return lax.all_to_all(blocks, axes, 0, 0, tiled=True)  74.4 us
    ppermute x6, waiting for transfers between devices, shifted(): return lax.ppermute(block, CTX, [((i - distance) % n, i) for i in range(n)])  52.8 us
    ppermute x6, starting transfers between devices, shifted(): return lax.ppermute(block, CTX, [((i - distance) % n, i) for i in range(n)])  26.7 us
    ppermute x1, starting transfers between devices, on_device(): other = lax.ppermute(summed, ('zh',), [(i, 1 - i) for i in range(nzh)])  14.8 us
    pallas_call x1, Pallas kernels, attention(): pl.pallas_call(attention_kernel, grid=(KEY_VALUE_HEADS,), in_specs=[pl.Bl...  8.32 us
    all_to_all x1, starting transfers between devices, exchange(): return lax.all_to_all(blocks, axes, 0, 0, tiled=True)  7.76 us
  transfers between devices with their start and end apart: 8, of which 4 were waited for; matrix products, arithmetic and copies ran while one was open for 0% of the time, Pallas kernels for 4%

profile of v2, /device:TPU:1, one launch (start us, length us, event | category | flops | bytes accessed | tf_op | source)
XLA Modules:
  0.0 204.7 jit_solution(9298865977625775704)
XLA Ops:
  0.6 2.9 %squeeze.17 = bf16[128,4,1280]{2,1,0:T(4,128)(2,1)S(1)} reshape(bf16[1,128,5120]{2,1,0:T(8,128)(2,1)} %param.11) | data formatting | bytes 2621440 | tf_op jit(solution)/shard_map/inputs_exchange/reshape;inputs_exchange/squeeze | solution.py:154
  3.5 0.1 copy.22
  3.6 2.9 %broadcast_in_dim.32 = bf16[4,4,128,1280]{3,2,1,0:T(8,128)(2,1)} broadcast(bf16[4,128,1280]{2,1,0:T(8,128)(2,1)S(1)} %copy.22), dimensions={0,2,3} | broadcast | bytes 6553600 | tf_op jit(solution)/shard_map/inputs_exchange/broadcast_in_dim | solution.py:155
  6.5 0.0 copy-start.8
  6.5 0.0 copy-start.3
  6.5 7.8 %all-to-all-start = ((bf16[16,128,1280]{2,1,0:T(8,128)(2,1)}), bf16[16,128,1280]{2,1,0:T(8,128)(2,1)}, u32[]{:S(2)}, u32[]{:S(2)}) async-start(bf16[16,128,1280]{2,1,0:T(8,128)(2,1)} %bitcast.31), calls=%async_computation | async-start | bytes 10485760 | tf_op jit(solution)/shard_map/inputs_exchange/all_to_all | solution.py:33
  14.3 0.0 copy-done.8
  14.3 0.1 broadcast_in_dim.14
  14.4 0.1 reshape.44
  14.5 0.0 copy-done.3
  14.5 0.0 copy-done.4
  14.5 0.1 maximum_maximum_fusion
  14.6 6.3 %collective-permute-start.2 = (bf16[272,512]{1,0:T(8,128)(2,1)S(1)}, bf16[272,512]{1,0:T(8,128)(2,1)S(1)}, u32[]{:S(2)}, u32[]{:S(2)}) collective-permute-start(bf16[272,512]{1,0:T(8,128)(2,1)S(1)} %maximum_maximum_fusion), channel_id=1, source_target_pairs={{464,0},{480,16},{496,32},{0,48},{16,64},{32,80},{48,96},{64,112},... | collective-permute-start | bytes 835592 | tf_op jit(solution)/shard_map/keys_values_halo/ppermute | solution.py:29
  20.8 6.1 %collective-permute-start.1 = (bf16[272,512]{1,0:T(8,128)(2,1)S(1)}, bf16[272,512]{1,0:T(8,128)(2,1)S(1)}, u32[]{:S(2)}, u32[]{:S(2)}) collective-permute-start(bf16[272,512]{1,0:T(8,128)(2,1)S(1)} %maximum_maximum_fusion), channel_id=1, source_target_pairs={{480,0},{496,16},{0,32},{16,48},{32,64},{48,80},{64,96},{80,112},{... | collective-permute-start | bytes 835592 | tf_op jit(solution)/shard_map/keys_values_halo/ppermute | solution.py:29
  27.0 3.5 %collective-permute-start = (bf16[272,512]{1,0:T(8,128)(2,1)S(1)}, bf16[272,512]{1,0:T(8,128)(2,1)S(1)}, u32[]{:S(2)}, u32[]{:S(2)}) collective-permute-start(bf16[272,512]{1,0:T(8,128)(2,1)S(1)} %maximum_maximum_fusion), channel_id=1, source_target_pairs={{496,0},{0,16},{16,32},{32,48},{48,64},{64,80},{80,96},{96,112},{1... | collective-permute-start | bytes 835592 | tf_op jit(solution)/shard_map/keys_values_halo/ppermute | solution.py:29
  30.5 32.3 %collective-permute-done.2.t3_ref = bf16[272,512]{1,0:T(8,128)(2,1)S(1)} collective-permute-done((bf16[272,512]{1,0:T(8,128)(2,1)S(1)}, bf16[272,512]{1,0:T(8,128)(2,1)S(1)}, u32[]{:S(2)}, u32[]{:S(2)}) %collective-permute-start.2) | collective-permute-done | bytes 278560 | tf_op jit(solution)/shard_map/keys_values_halo/ppermute | solution.py:29
  62.8 0.0 collective-permute-done.1.t2_ref
  62.8 0.0 collective-permute-done.t1_ref
  62.8 0.7 copy-done.5
  63.5 0.1 copy-done.6
  63.6 0.7 copy-done.7
  64.3 8.3 %attention.1 = (bf16[1,128,2560]{2,1,0:T(8,128)(2,1)}, f32[2,2,128,256]{3,2,1,0:T(8,128)}, bf16[2,2,128,256]{3,2,1,0:T(8,128)(2,1)}, bf16[2,2,128,256]{3,2,1,0:T(8,128)(2,1)}, bf16[2,2,128,256]{3,2,1,0:T(8,128)(2,1)}) custom-call(s32[2]{0:T(128)} %span_ref.1, s32[1,4096]{1,0:T(1,128)} %seg_ref.1, bf16[1,128,2560]{2,1,0:T(8,128)(2,1)} %q_ref.1, ...), custom_call_target="tpu_custom_call" | custom-call | flops 1677721600 | bytes 5242880 | tf_op jit(solution)/shard_map/attention/attention/pallas_call | solution.py:120
  72.7 1.9 collective-permute-start.3
  74.6 7.0 %collective-permute-start.4 = (bf16[2,2,128,256]{3,2,1,0:T(8,128)(2,1)}, bf16[2,2,128,256]{3,2,1,0:T(8,128)(2,1)S(1)}, u32[]{:S(2)}, u32[]{:S(2)}) collective-permute-start(bf16[2,2,128,256]{3,2,1,0:T(8,128)(2,1)} %get-tuple-element.11), channel_id=1, source_target_pairs={{32,0},{48,16},{64,32},{80,48},{96,64},{112,80},{128,96},{144,112}... | collective-permute-start | bytes 786440 | tf_op jit(solution)/shard_map/gradient_return/ppermute | solution.py:29
  81.5 1.9 collective-permute-start.5
  83.5 0.0 collective-permute-done.3.b1_ref
  83.5 0.0 copy-start
  83.5 6.1 %collective-permute-done.4.b2_ref = bf16[2,2,128,256]{3,2,1,0:T(8,128)(2,1)S(1)} collective-permute-done((bf16[2,2,128,256]{3,2,1,0:T(8,128)(2,1)}, bf16[2,2,128,256]{3,2,1,0:T(8,128)(2,1)S(1)}, u32[]{:S(2)}, u32[]{:S(2)}) %collective-permute-start.4) | collective-permute-done | bytes 262176 | tf_op jit(solution)/shard_map/gradient_return/ppermute | solution.py:29
  89.6 14.5 %collective-permute-done.5.b3_ref = bf16[2,2,128,256]{3,2,1,0:T(8,128)(2,1)S(1)} collective-permute-done((bf16[2,2,128,256]{3,2,1,0:T(8,128)(2,1)}, bf16[2,2,128,256]{3,2,1,0:T(8,128)(2,1)S(1)}, u32[]{:S(2)}, u32[]{:S(2)}) %collective-permute-start.5) | collective-permute-done | bytes 262176 | tf_op jit(solution)/shard_map/gradient_return/ppermute | solution.py:29
  104.0 0.0 all-to-all-done
  104.0 0.0 copy-done
  104.0 0.0 copy-done.1
  104.0 0.7 copy-done.2
  104.7 2.1 %sum_terms.1 = bf16[2,2,128,256]{3,2,1,0:T(8,128)(2,1)} custom-call(f32[2,2,128,256]{3,2,1,0:T(8,128)} %get-tuple-element.9.own_ref, bf16[2,2,128,256]{3,2,1,0:T(8,128)(2,1)} %copy-done, bf16[2,2,128,256]{3,2,1,0:T(8,128)(2,1)} %copy-done.1, bf16[2,2,128,256]{3,2,1,0:T(8,128)(2,1)} %copy-done.2, bf16[2048,1280]{1,0:T(8,128)(2,1)} %bitcast.4.after_ref), custom_call_target="tpu_custom_call" | custom-call | flops 524288 | bytes 2359296 | tf_op jit(solution)/shard_map/gradient_return/sum_terms/pallas_call | solution.py:103
  106.8 1.1 copy.23
  107.9 0.2 broadcast_in_dim.34
  108.1 19.7 %all_to_all.25 = bf16[16,128,256]{1,2,0:T(8,128)(2,1)S(1)} all-to-all(bf16[16,128,256]{1,2,0:T(8,128)(2,1)S(1)} %bitcast.33), channel_id=1, replica_groups=mesh['x'=4,'zl'=8,'y'=4,'zh'=2,'c'=2] {'x','y'}, dimensions={0} | all-to-all | bytes 2097152 | tf_op jit(solution)/shard_map/gradient_exchange/all_to_all | solution.py:33
  127.8 4.1 %fusion = bf16[256,1280]{1,0:T(8,128)(2,1)S(1)} fusion(bf16[16,128,256]{1,2,0:T(8,128)(2,1)S(1)} %all_to_all.25, bf16[16,128,1280]{2,1,0:T(8,128)(2,1)} %all-to-all-done), kind=kOutput, calls=%fused_computation.1 | convolution fusion | flops 1342504960 | bytes 6946816 | tf_op jit(solution)/shard_map/projection/dot_general | solution.py:37
  131.9 7.4 %all_to_all.26 = bf16[2,1280,128]{1,2,0:T(8,128)(2,1)S(1)} all-to-all(bf16[2,1280,128]{1,2,0:T(8,128)(2,1)S(1)} %bitcast.39), channel_id=1, replica_groups=mesh['x'=4,'zl'=8,'y'=4,'zh'=2,'c'=2] {'c'}, dimensions={0} | all-to-all | bytes 1310720 | tf_op jit(solution)/shard_map/core_sum/all_to_all | solution.py:33
  139.3 0.1 reduce_sum.24
  139.5 0.2 copy.24
  139.7 34.3 %all_to_all.27 = bf16[8,160,128]{2,1,0:T(8,128)(2,1)S(1)} all-to-all(bf16[8,160,128]{2,1,0:T(8,128)(2,1)S(1)} %bitcast.36), channel_id=1, replica_groups=mesh['x'=4,'zl'=8,'y'=4,'zh'=2,'c'=2] {'zl'}, dimensions={0} | all-to-all | bytes 655360 | tf_op jit(solution)/shard_map/z_sum/all_to_all | solution.py:33
  174.1 14.8 %collective-permute-start.6 = (bf16[160,128]{1,0:T(8,128)(2,1)S(1)}, bf16[160,128]{1,0:T(8,128)(2,1)S(1)}, u32[]{:S(2)}, u32[]{:S(2)}) collective-permute-start(bf16[160,128]{1,0:T(8,128)(2,1)S(1)} %reduce_sum.25), channel_id=1, source_target_pairs={{0,2},{2,0},{1,3},{3,1},{4,6},{6,4},{5,7},{7,5},{8,10},{10,8},{9,1... | collective-permute-start | bytes 122888 | tf_op jit(solution)/shard_map/z_sum/ppermute | solution.py:177
  188.9 1.4 collective-permute-done.6
  190.3 12.9 %all_to_all.28 = bf16[8,160,128]{2,1,0:T(8,128)(2,1)S(1)} all-to-all(bf16[8,160,128]{2,1,0:T(8,128)(2,1)S(1)} %broadcast_in_dim.35), channel_id=1, replica_groups=mesh['x'=4,'zl'=8,'y'=4,'zh'=2,'c'=2] {'y','c'}, dimensions={0} | all-to-all | bytes 655360 | tf_op jit(solution)/shard_map/replicate/all_to_all | solution.py:33
  203.3 0.2 copy.26
  203.6 0.2 copy.25
  203.8 0.9 copy_bitcast_fusion
  (13 shorter events, 0.2 us)
Async XLA Ops:
  6.5 7.8 %copy-start.8 = (s32[2]{0:T(128)S(1)}, s32[2]{0:T(128)}, u32[]{:S(2)}) copy-start(s32[2]{0:T(128)} %span_ref.1) | copy-start | bytes 28
  6.5 8.0 %copy-start.3 = (bf16[1,128,512]{2,1,0:T(8,128)(2,1)S(1)}, bf16[1,128,512]{2,1,0:T(8,128)(2,1)}, u32[]{:S(2)}) copy-start(bf16[1,128,512]{2,1,0:T(8,128)(2,1)} %k_ref.1) | copy-start | bytes 393220
  6.5 8.0 %copy-start.4 = (bf16[1,128,512]{2,1,0:T(8,128)(2,1)S(1)}, bf16[1,128,512]{2,1,0:T(8,128)(2,1)}, u32[]{:S(2)}) copy-start(bf16[1,128,512]{2,1,0:T(8,128)(2,1)} %v_ref.1) | copy-start | bytes 393220
  6.5 97.5 %all-to-all-start = ((bf16[16,128,1280]{2,1,0:T(8,128)(2,1)}), bf16[16,128,1280]{2,1,0:T(8,128)(2,1)}, u32[]{:S(2)}, u32[]{:S(2)}) async-start(bf16[16,128,1280]{2,1,0:T(8,128)(2,1)} %bitcast.31), calls=%async_computation | async-start | bytes 10485760 | tf_op jit(solution)/shard_map/inputs_exchange/all_to_all | solution.py:33
  14.6 48.2 %collective-permute-start.2 = (bf16[272,512]{1,0:T(8,128)(2,1)S(1)}, bf16[272,512]{1,0:T(8,128)(2,1)S(1)}, u32[]{:S(2)}, u32[]{:S(2)}) collective-permute-start(bf16[272,512]{1,0:T(8,128)(2,1)S(1)} %maximum_maximum_fusion), channel_id=1, source_target_pairs={{464,0},{480,16},{496,32},{0,48},{16,64},{32,80},{48,96},{64,112},... | collective-permute-start | bytes 835592 | tf_op jit(solution)/shard_map/keys_values_halo/ppermute | solution.py:29
  20.8 42.0 %collective-permute-start.1 = (bf16[272,512]{1,0:T(8,128)(2,1)S(1)}, bf16[272,512]{1,0:T(8,128)(2,1)S(1)}, u32[]{:S(2)}, u32[]{:S(2)}) collective-permute-start(bf16[272,512]{1,0:T(8,128)(2,1)S(1)} %maximum_maximum_fusion), channel_id=1, source_target_pairs={{480,0},{496,16},{0,32},{16,48},{32,64},{48,80},{64,96},{80,112},{... | collective-permute-start | bytes 835592 | tf_op jit(solution)/shard_map/keys_values_halo/ppermute | solution.py:29
  27.0 35.9 %collective-permute-start = (bf16[272,512]{1,0:T(8,128)(2,1)S(1)}, bf16[272,512]{1,0:T(8,128)(2,1)S(1)}, u32[]{:S(2)}, u32[]{:S(2)}) collective-permute-start(bf16[272,512]{1,0:T(8,128)(2,1)S(1)} %maximum_maximum_fusion), channel_id=1, source_target_pairs={{496,0},{0,16},{16,32},{32,48},{48,64},{64,80},{80,96},{96,112},{1... | collective-permute-start | bytes 835592 | tf_op jit(solution)/shard_map/keys_values_halo/ppermute | solution.py:29
  62.8 0.7 copy-start.5
  62.8 0.8 copy-start.6
  63.6 0.7 copy-start.7
  72.7 10.8 %collective-permute-start.3 = (bf16[2,2,128,256]{3,2,1,0:T(8,128)(2,1)}, bf16[2,2,128,256]{3,2,1,0:T(8,128)(2,1)S(1)}, u32[]{:S(2)}, u32[]{:S(2)}) collective-permute-start(bf16[2,2,128,256]{3,2,1,0:T(8,128)(2,1)} %get-tuple-element.10), channel_id=1, source_target_pairs={{16,0},{32,16},{48,32},{64,48},{80,64},{96,80},{112,96},{128,112},... | collective-permute-start | bytes 786440 | tf_op jit(solution)/shard_map/gradient_return/ppermute | solution.py:29
  74.6 15.0 %collective-permute-start.4 = (bf16[2,2,128,256]{3,2,1,0:T(8,128)(2,1)}, bf16[2,2,128,256]{3,2,1,0:T(8,128)(2,1)S(1)}, u32[]{:S(2)}, u32[]{:S(2)}) collective-permute-start(bf16[2,2,128,256]{3,2,1,0:T(8,128)(2,1)} %get-tuple-element.11), channel_id=1, source_target_pairs={{32,0},{48,16},{64,32},{80,48},{96,64},{112,80},{128,96},{144,112}... | collective-permute-start | bytes 786440 | tf_op jit(solution)/shard_map/gradient_return/ppermute | solution.py:29
  81.5 22.5 %collective-permute-start.5 = (bf16[2,2,128,256]{3,2,1,0:T(8,128)(2,1)}, bf16[2,2,128,256]{3,2,1,0:T(8,128)(2,1)S(1)}, u32[]{:S(2)}, u32[]{:S(2)}) collective-permute-start(bf16[2,2,128,256]{3,2,1,0:T(8,128)(2,1)} %get-tuple-element.12), channel_id=1, source_target_pairs={{48,0},{64,16},{80,32},{96,48},{112,64},{128,80},{144,96},{160,112... | collective-permute-start | bytes 786440 | tf_op jit(solution)/shard_map/gradient_return/ppermute | solution.py:29
  83.5 20.5 %copy-start = (bf16[2,2,128,256]{3,2,1,0:T(8,128)(2,1)}, bf16[2,2,128,256]{3,2,1,0:T(8,128)(2,1)S(1)}, u32[]{:S(2)}) copy-start(bf16[2,2,128,256]{3,2,1,0:T(8,128)(2,1)S(1)} %collective-permute-done.3.b1_ref) | copy-start | bytes 786436
  89.6 14.5 %copy-start.1 = (bf16[2,2,128,256]{3,2,1,0:T(8,128)(2,1)}, bf16[2,2,128,256]{3,2,1,0:T(8,128)(2,1)S(1)}, u32[]{:S(2)}) copy-start(bf16[2,2,128,256]{3,2,1,0:T(8,128)(2,1)S(1)} %collective-permute-done.4.b2_ref) | copy-start | bytes 786436
  104.0 0.7 copy-start.2
  174.1 16.2 %collective-permute-start.6 = (bf16[160,128]{1,0:T(8,128)(2,1)S(1)}, bf16[160,128]{1,0:T(8,128)(2,1)S(1)}, u32[]{:S(2)}, u32[]{:S(2)}) collective-permute-start(bf16[160,128]{1,0:T(8,128)(2,1)S(1)} %reduce_sum.25), channel_id=1, source_target_pairs={{0,2},{2,0},{1,3},{3,1},{4,6},{6,4},{5,7},{7,5},{8,10},{10,8},{9,1... | collective-permute-start | bytes 122888 | tf_op jit(solution)/shard_map/z_sum/ppermute | solution.py:177

commit v3 on v2

--- a/solution.py
+++ b/solution.py
@@ -17,7 +17,8 @@
 WINDOW = 4
 DOCUMENTS = 8
 SCALE = HEAD ** (-0.5)
-CTX = ("x", "zl")
+LINE = ("za", "zb")
+CTX = ("x",) + LINE
 DP = ("y", "zh", "c")
 BF16 = jnp.bfloat16
 VMEM_LIMIT = 60 * 1024 * 1024
@@ -27,6 +28,21 @@
 def shifted(block, distance):
     n = lax.axis_size(CTX)
     return lax.ppermute(block, CTX, [((i - distance) % n, i) for i in range(n)])
+
+
+def beyond(block, second):
+    nx, nz = lax.axis_size("x"), lax.axis_size(LINE)
+    across = lax.ppermute(block, CTX, [(x * nz + nz - 3, (x + 1) % nx * nz) for x in range(nx)])
+    along = lax.ppermute(second, LINE, [(z, z + 1) for z in range(nz - 1)])
+    return jnp.where(lax.axis_index(LINE) == 0, across, along)
+
+
+def returned(first, second, third):
+    nx, nz = lax.axis_size("x"), lax.axis_size(LINE)
+    along = lax.ppermute(third, LINE, [(z, z - 1) for z in range(1, nz)])
+    across = lax.ppermute(third, CTX, [(x * nz, (x - 1) % nx * nz + nz - 3) for x in range(nx)])
+    second = (second.astype(F32) + along.astype(F32)).astype(BF16)
+    return shifted(first, -1), shifted(second, -2), across
 
 
 def exchange(blocks, axes):
@@ -90,22 +106,82 @@
         ref[1] = dv[rows].astype(BF16)
 
 
+def tile_kernel(span_ref, k_ref, v_ref, tile_ref):
+    tile_ref[0:ROWS, :] = k_ref[0]
+    tile_ref[ROWS : 2 * ROWS, :] = v_ref[0]
+    row = lax.broadcasted_iota(jnp.int32, (16, tile_ref.shape[1]), 0)
+    number = jnp.where(row < 8, span_ref[0], span_ref[1]).astype(F32)
+    tile_ref[2 * ROWS :, :] = number.astype(BF16)
+
+
+def packed_tile(span, keys, values):
+    whole = pl.BlockSpec(memory_space=pltpu.VMEM)
+    return pl.pallas_call(
+        tile_kernel,
+        in_specs=[pl.BlockSpec(memory_space=pltpu.SMEM), whole, whole],
+        out_specs=whole,
+        out_shape=jax.ShapeDtypeStruct((2 * ROWS + 16, keys.shape[2]), BF16),
+        compiler_params=pltpu.CompilerParams(vmem_limit_bytes=VMEM_LIMIT),
+        name="packed_tile",
+    )(span, keys, values)
+
+
+def copies_kernel(x_ref, out_ref, sems):
+    parts = x_ref.shape[2] // out_ref.shape[2]
+    copies = out_ref.shape[0] // parts
+    width = out_ref.shape[2]
+    moves = [
+        pltpu.make_async_copy(
+            x_ref.at[0, :, i * width : (i + 1) * width], out_ref.at[i * copies + j], sems.at[i, j]
+        )
+        for i in range(parts)
+        for j in range(copies)
+    ]
+    for move in moves:
+        move.start()
+    for move in moves:
+        move.wait()
+
+
+def feature_blocks(inputs, parts, copies):
+    rows, features = inputs.shape[1:]
+    return pl.pallas_call(
+        copies_kernel,
+        in_specs=[pl.BlockSpec(memory_space=pltpu.VMEM)],
+        out_specs=pl.BlockSpec(memory_space=pl.ANY),
+        out_shape=jax.ShapeDtypeStruct((parts * copies, rows, features // parts), BF16),
+        scratch_shapes=[pltpu.SemaphoreType.DMA((parts, copies))],
+        compiler_params=pltpu.CompilerParams(vmem_limit_bytes=VMEM_LIMIT),
+        cost_estimate=pl.CostEstimate(
+            flops=0, bytes_accessed=4 * rows * features * copies, transcendentals=0
+        ),
+        name="feature_blocks",
+    )(inputs)
+
+
 def sum_kernel(own_ref, b1_ref, b2_ref, b3_ref, after_ref, out_ref):
     del after_ref
     total = own_ref[...]
     for ref in (b1_ref, b2_ref, b3_ref):
         total = total + ref[...].astype(F32)
-    out_ref[...] = total.astype(BF16)
-
-
-def sum_terms(own, back, after):
+    for i in range(2):
+        for j in range(2):
+            turned = total[i, j].T.astype(BF16)
+            for copy in range(out_ref.shape[0]):
+                out_ref[copy, 2 * i + j] = turned
+
+
+def sum_terms(own, back, copies, after):
     whole = pl.BlockSpec(memory_space=pltpu.VMEM)
     return pl.pallas_call(
         sum_kernel,
         in_specs=[whole] * 4 + [pl.BlockSpec(memory_space=pl.ANY)],
         out_specs=whole,
-        out_shape=jax.ShapeDtypeStruct(own.shape, BF16),
-        cost_estimate=pl.CostEstimate(flops=own.size * 4, bytes_accessed=own.size * 18, transcendentals=0),
+        out_shape=jax.ShapeDtypeStruct((copies, 4, own.shape[3], own.shape[2]), BF16),
+        compiler_params=pltpu.CompilerParams(vmem_limit_bytes=VMEM_LIMIT),
+        cost_estimate=pl.CostEstimate(
+            flops=own.size * 4, bytes_accessed=own.size * 18, transcendentals=0
+        ),
         name="sum_terms",
     )(own, *back, after)
 
@@ -143,39 +219,38 @@
 
 
 def on_device(queries, keys, values, output_gradient, inputs, span_ids, segments):
-    nx, ny, nzl, nzh, nc = (lax.axis_size(a) for a in ("x", "y", "zl", "zh", "c"))
+    nx, ny, na, nb, nzh, nc = (lax.axis_size(a) for a in ("x", "y", "za", "zb", "zh", "c"))
     rows, features = inputs.shape[1:]
     part = features // nx
     with jax.named_scope("keys_values_halo"):
-        numbers = jnp.broadcast_to(span_ids.astype(BF16)[:, None, None], (2, 8, keys.shape[2]))
-        tile = jnp.concatenate([keys[0], values[0], numbers.reshape(16, keys.shape[2])], axis=0)
-        tiles = [shifted(tile, step) for step in range(1, WINDOW)]
+        tile = packed_tile(span_ids, keys, values)
+        tiles = [shifted(tile, 1), shifted(tile, 2)]
+        tiles.append(beyond(tile, lax.optimization_barrier((tiles[1], tiles[0]))[0]))
     with jax.named_scope("inputs_exchange"):
-        by_x = inputs[0].reshape(rows, nx, part).transpose(1, 0, 2)
-        blocks = jnp.broadcast_to(by_x[:, None], (nx, ny, rows, part)).reshape(nx * ny, rows, part)
-        features_x = exchange(blocks, ("x", "y")).reshape(nx * ny * rows, part)
+        blocks = feature_blocks(inputs, nx, ny)
+        features_x = exchange(blocks, ("x", "y"))
     with jax.named_scope("attention"):
         grad_queries, own, *terms = attention(
             span_ids, segments, queries, output_gradient, keys, values, tiles
         )
     with jax.named_scope("gradient_return"):
-        back = [shifted(term, -step) for step, term in enumerate(terms, 1)]
-        blocks = sum_terms(own, back, features_x)
+        back = returned(*terms)
+        blocks = sum_terms(own, back, nx, features_x)
     with jax.named_scope("gradient_exchange"):
-        blocks = jnp.broadcast_to(blocks.reshape(ny, rows, 2 * HEAD)[None], (nx, ny, rows, 2 * HEAD))
-        columns = exchange(blocks.reshape(nx * ny, rows, 2 * HEAD), ("x", "y"))
-        columns = columns.reshape(nx * ny * rows, 2 * HEAD)
+        columns = exchange(blocks.reshape(nx * ny, 2 * HEAD, rows), ("x", "y"))
     with jax.named_scope("projection"):
-        partial = dot(features_x, columns, 0, 0)
+        partial = jnp.einsum("bcr,brf->cf", columns, features_x, preferred_element_type=F32)
     with jax.named_scope("core_sum"):
-        halves = partial.astype(BF16).reshape(part, nc, HEAD).transpose(1, 0, 2)
-        pair = jnp.sum(exchange(halves, ("c",)).astype(F32), axis=0)
+        halves = exchange(partial.astype(BF16).reshape(nc, HEAD, part), ("c",))
+        pair = jnp.sum(halves.astype(F32), axis=0).astype(BF16)
     with jax.named_scope("z_sum"):
-        piece = part // nzl
-        pieces = exchange(pair.astype(BF16).reshape(nzl, piece, HEAD), ("zl",))
+        piece = part // (na * nb)
+        pieces = pair.T.reshape(na, nb, piece, HEAD).transpose(1, 0, 2, 3)
+        pieces = exchange(pieces, ("zb",))
         summed = jnp.sum(pieces.astype(F32), axis=0).astype(BF16)
-        other = lax.ppermute(summed, ("zh",), [(i, 1 - i) for i in range(nzh)])
-        summed = (summed.astype(F32) + other.astype(F32)).astype(BF16)
+        pieces = jnp.broadcast_to(summed[None], (nzh, na, piece, HEAD))
+        pieces = exchange(pieces.reshape(nzh * na, piece, HEAD), ("zh", "za"))
+        summed = jnp.sum(pieces.astype(F32), axis=0).astype(BF16)
     with jax.named_scope("replicate"):
         every = exchange(jnp.broadcast_to(summed[None], (ny * nc, piece, HEAD)), ("y", "c"))
         every = every.reshape(2, ny * nc // 2, piece, HEAD).transpose(0, 2, 1, 3).astype(F32)
@@ -184,7 +259,7 @@
 
 
 def solution(mesh):
-    axes = Mesh(mesh.devices.reshape(4, 8, 4, 2, 2), CTX + DP)
+    axes = Mesh(mesh.devices.reshape(4, 2, 4, 4, 2, 2), CTX + DP)
     by_row = P(DP, CTX, None)
     return jax.shard_map(
         on_device,

time: 205 us -> 187 us (0.912)
  waiting for transfers between devices: 54.2 us -> 37.9 us
  starting transfers between devices: 49.2 us -> 35.7 us
  blocking collectives: 74.4 us -> 87.1 us
  local copies, waits for them, and re-layouts: 11.1 us -> 2.35 us
  Pallas kernels: 10.4 us -> 16.3 us
    ppermute x6 -> x4, waiting for transfers between devices: 52.8 us -> 31.9 us  [shifted(): return lax.ppermute(block, CTX, [((i - distance) % n, i) for i in range(n)])]
    all_to_all x4 -> x5, blocking collectives: 74.4 us -> 87.1 us  [exchange(): return lax.all_to_all(blocks, axes, 0, 0, tiled=True)]
    ppermute x6 -> x4, starting transfers between devices: 26.7 us -> 14.5 us  [shifted(): return lax.ppermute(block, CTX, [((i - distance) % n, i) for i in range(n)])]
    pallas_call x0 -> x2, Pallas kernels: none -> 5.5 us  [the longest x1 3.79 us: feature_blocks(): pl.pallas_call(copies_kernel, in_specs=[pl.BlockSpec(memory_space=pltpu.V...]
    ppermute x1 -> x4, waiting for transfers between devices: 1.38 us -> 6.03 us  [the longest x1 6.02 us: beyond(): lax.ppermute(block, CTX, [(x * nz + nz - 3, (x + 1) % nx * nz) for x in r...]
    broadcast_in_dim x5 -> x1, local copies, waits for them, and re-layouts: 4.33 us -> 0.02 us  [on_device(): pieces = jnp.broadcast_to(summed[None], (nzh, na, piece, HEAD))]
    squeeze x1 -> x0, local copies, waits for them, and re-layouts: 2.86 us -> none  [on_device(): by_x = inputs[0].reshape(rows, nx, part).transpose(1, 0, 2)]
    ppermute x1 -> x4, starting transfers between devices: 14.8 us -> 13.6 us  [the longest x1 9.75 us: returned(): lax.ppermute(third, CTX, [(x * nz, (x - 1) % nx * nz + nz - 3) for x in r...]
  transfers between devices with their start and end apart: 8 -> 9, of which waited for: 4 -> 4; matrix products, arithmetic and copies ran while one was open for 0% -> 1% of each run, Pallas kernels for 4% -> 5%
where the time goes in v3:
time: 187 us; the launch traced here: 186 us
  blocking collectives  87.1 us (47%)
  waiting for transfers between devices  37.9 us (20%)
  starting transfers between devices  35.7 us (19%)
  Pallas kernels  16.3 us (9%)
  matrix products  4.07 us (2%)
  local copies, waits for them, and re-layouts  2.35 us (1%)
  other arithmetic  2.03 us (1%)
    all_to_all x5, blocking collectives, exchange(): return lax.all_to_all(blocks, axes, 0, 0, tiled=True)  87.1 us
    ppermute x4, waiting for transfers between devices, shifted(): return lax.ppermute(block, CTX, [((i - distance) % n, i) for i in range(n)])  31.9 us
    ppermute x4, starting transfers between devices, shifted(): return lax.ppermute(block, CTX, [((i - distance) % n, i) for i in range(n)])  14.5 us
    ppermute x1, starting transfers between devices, returned(): lax.ppermute(third, CTX, [(x * nz, (x - 1) % nx * nz + nz - 3) for x in r...  9.75 us
    pallas_call x1, Pallas kernels, attention(): pl.pallas_call(attention_kernel, grid=(KEY_VALUE_HEADS,), in_specs=[pl.Bl...  8.33 us
    all_to_all x1, starting transfers between devices, exchange(): return lax.all_to_all(blocks, axes, 0, 0, tiled=True)  7.64 us
    ppermute x1, waiting for transfers between devices, beyond(): lax.ppermute(block, CTX, [(x * nz + nz - 3, (x + 1) % nx * nz) for x in r...  6.02 us
    dot_general x1, matrix products, on_device(): jnp.einsum('bcr,brf->cf', columns, features_x, preferred_element_type=F32)  4.07 us
  transfers between devices with their start and end apart: 9, of which 4 were waited for; matrix products, arithmetic and copies ran while one was open for 1% of the time, Pallas kernels for 5%

profile of v3, /device:TPU:1, one launch (start us, length us, event | category | flops | bytes accessed | tf_op | source)
XLA Modules:
  0.0 186.4 jit_solution(15504054679990004746)
XLA Ops:
  0.6 3.8 %feature_blocks.1 = bf16[16,128,1280]{2,1,0:T(8,128)(2,1)} custom-call(bf16[1,128,5120]{2,1,0:T(8,128)(2,1)} %x_ref.1), custom_call_target="tpu_custom_call" | custom-call | bytes 10485760 | tf_op jit(solution)/shard_map/inputs_exchange/feature_blocks/pallas_call | solution.py:148
  4.4 7.6 %all-to-all-start = ((bf16[16,128,1280]{2,1,0:T(8,128)(2,1)}), bf16[16,128,1280]{2,1,0:T(8,128)(2,1)}, u32[]{:S(2)}, u32[]{:S(2)}) async-start(bf16[16,128,1280]{2,1,0:T(8,128)(2,1)} %feature_blocks.1), calls=%async_computation | async-start | bytes 10485760 | tf_op jit(solution)/shard_map/inputs_exchange/all_to_all | solution.py:49
  12.1 1.7 packed_tile.1
  13.8 4.9 %collective-permute-start.1 = (bf16[272,512]{1,0:T(8,128)(2,1)}, bf16[272,512]{1,0:T(8,128)(2,1)S(1)}, u32[]{:S(2)}, u32[]{:S(2)}) collective-permute-start(bf16[272,512]{1,0:T(8,128)(2,1)} %packed_tile.1), channel_id=1, source_target_pairs={{480,0},{496,16},{0,32},{16,48},{32,64},{48,80},{64,96},{80,112},{... | collective-permute-start | bytes 835592 | tf_op jit(solution)/shard_map/keys_values_halo/ppermute | solution.py:30
  18.7 3.5 %collective-permute-start = (bf16[272,512]{1,0:T(8,128)(2,1)}, bf16[272,512]{1,0:T(8,128)(2,1)S(1)}, u32[]{:S(2)}, u32[]{:S(2)}) collective-permute-start(bf16[272,512]{1,0:T(8,128)(2,1)} %packed_tile.1), channel_id=1, source_target_pairs={{496,0},{0,16},{16,32},{32,48},{48,64},{64,80},{80,96},{96,112},{1... | collective-permute-start | bytes 835592 | tf_op jit(solution)/shard_map/keys_values_halo/ppermute | solution.py:30
  22.2 1.3 collective-permute-start.2
  23.5 21.9 %collective-permute-done.1.t2_ref = bf16[272,512]{1,0:T(8,128)(2,1)S(1)} collective-permute-done((bf16[272,512]{1,0:T(8,128)(2,1)}, bf16[272,512]{1,0:T(8,128)(2,1)S(1)}, u32[]{:S(2)}, u32[]{:S(2)}) %collective-permute-start.1) | collective-permute-done | bytes 278560 | tf_op jit(solution)/shard_map/keys_values_halo/ppermute | solution.py:30
  45.4 0.0 copy-start.3
  45.4 0.0 collective-permute-done.t1_ref
  45.4 0.0 copy-start.4
  45.4 1.3 collective-permute-start.3
  46.8 6.0 %collective-permute-done.2 = bf16[272,512]{1,0:T(8,128)(2,1)S(1)} collective-permute-done((bf16[272,512]{1,0:T(8,128)(2,1)}, bf16[272,512]{1,0:T(8,128)(2,1)S(1)}, u32[]{:S(2)}, u32[]{:S(2)}) %collective-permute-start.2) | collective-permute-done | bytes 278560 | tf_op jit(solution)/shard_map/keys_values_halo/ppermute | solution.py:35
  52.8 0.0 collective-permute-done.3
  52.8 0.7 broadcast_select_fusion.t3_ref
  53.5 0.0 copy-done.3
  53.5 0.0 copy-done.4
  53.5 8.3 %attention.1 = (bf16[1,128,2560]{2,1,0:T(8,128)(2,1)}, f32[2,2,128,256]{3,2,1,0:T(8,128)}, bf16[2,2,128,256]{3,2,1,0:T(8,128)(2,1)}, bf16[2,2,128,256]{3,2,1,0:T(8,128)(2,1)}, bf16[2,2,128,256]{3,2,1,0:T(8,128)(2,1)}) custom-call(s32[2]{0:T(128)} %span_ref.3, s32[1,4096]{1,0:T(1,128)} %seg_ref.1, bf16[1,128,2560]{2,1,0:T(8,128)(2,1)} %q_ref.1, ...), custom_call_target="tpu_custom_call" | custom-call | flops 1677721600 | bytes 5242880 | tf_op jit(solution)/shard_map/attention/attention/pallas_call | solution.py:196
  61.9 1.3 collective-permute-start.5
  63.2 9.8 %collective-permute-start.7 = (bf16[2,2,128,256]{3,2,1,0:T(8,128)(2,1)}, bf16[2,2,128,256]{3,2,1,0:T(8,128)(2,1)S(1)}, u32[]{:S(2)}, u32[]{:S(2)}) collective-permute-start(bf16[2,2,128,256]{3,2,1,0:T(8,128)(2,1)} %get-tuple-element.14), channel_id=1, source_target_pairs={{0,464},{128,80},{256,208},{384,336},{1,465},{129,81},{257,209},{3... | collective-permute-start | bytes 786440 | tf_op jit(solution)/shard_map/gradient_return/ppermute | solution.py:43
  72.9 1.9 %collective-permute-start.4 = (bf16[2,2,128,256]{3,2,1,0:T(8,128)(2,1)}, bf16[2,2,128,256]{3,2,1,0:T(8,128)(2,1)S(1)}, u32[]{:S(2)}, u32[]{:S(2)}) collective-permute-start(bf16[2,2,128,256]{3,2,1,0:T(8,128)(2,1)} %get-tuple-element.12), channel_id=1, source_target_pairs={{16,0},{32,16},{48,32},{64,48},{80,64},{96,80},{112,96},{128,112},... | collective-permute-start | bytes 786440 | tf_op jit(solution)/shard_map/gradient_return/ppermute | solution.py:30
  74.8 0.0 collective-permute-done.5
  74.9 1.0 add_convert_fusion
  75.9 4.1 %collective-permute-start.6 = (bf16[2,2,128,256]{3,2,1,0:T(8,128)(2,1)S(1)}, bf16[2,2,128,256]{3,2,1,0:T(8,128)(2,1)S(1)}, u32[]{:S(2)}, u32[]{:S(2)}) collective-permute-start(bf16[2,2,128,256]{3,2,1,0:T(8,128)(2,1)S(1)} %add_convert_fusion), channel_id=1, source_target_pairs={{32,0},{48,16},{64,32},{80,48},{96,64},{112,80},{128,96},{144,112}... | collective-permute-start | bytes 786440 | tf_op jit(solution)/shard_map/gradient_return/ppermute | solution.py:30
  80.0 3.1 %collective-permute-done.4.b1_ref = bf16[2,2,128,256]{3,2,1,0:T(8,128)(2,1)S(1)} collective-permute-done((bf16[2,2,128,256]{3,2,1,0:T(8,128)(2,1)}, bf16[2,2,128,256]{3,2,1,0:T(8,128)(2,1)S(1)}, u32[]{:S(2)}, u32[]{:S(2)}) %collective-permute-start.4) | collective-permute-done | bytes 262176 | tf_op jit(solution)/shard_map/gradient_return/ppermute | solution.py:30
  83.1 0.0 copy-start.1
  83.1 0.0 collective-permute-done.7.b3_ref
  83.1 0.0 copy-start
  83.1 6.9 %collective-permute-done.6.b2_ref = bf16[2,2,128,256]{3,2,1,0:T(8,128)(2,1)S(1)} collective-permute-done((bf16[2,2,128,256]{3,2,1,0:T(8,128)(2,1)S(1)}, bf16[2,2,128,256]{3,2,1,0:T(8,128)(2,1)S(1)}, u32[]{:S(2)}, u32[]{:S(2)}) %collective-permute-start.6) | collective-permute-done | bytes 262176 | tf_op jit(solution)/shard_map/gradient_return/ppermute | solution.py:30
  90.0 0.0 copy-start.2
  90.0 0.0 all-to-all-done.after_ref
  90.0 0.0 copy-done.1
  90.0 0.0 copy-done
  90.0 0.7 copy-done.2
  90.7 2.5 %sum_terms.1 = bf16[4,4,256,128]{3,2,1,0:T(8,128)(2,1)} custom-call(f32[2,2,128,256]{3,2,1,0:T(8,128)} %get-tuple-element.11.own_ref, bf16[2,2,128,256]{3,2,1,0:T(8,128)(2,1)} %copy-done.1, bf16[2,2,128,256]{3,2,1,0:T(8,128)(2,1)} %copy-done.2, bf16[2,2,128,256]{3,2,1,0:T(8,128)(2,1)} %copy-done, bf16[16,128,1280]{2,1,0:T(8,128)(2,1)} %all-to-all-done.after_ref), custom_call_target="tpu_custom_call" | custom-call | flops 524288 | bytes 2359296 | tf_op jit(solution)/shard_map/gradient_return/sum_terms/pallas_call | solution.py:176
  93.2 19.7 %all_to_all.30 = bf16[16,256,128]{2,1,0:T(8,128)(2,1)S(1)} all-to-all(bf16[16,256,128]{2,1,0:T(8,128)(2,1)} %bitcast.25), channel_id=1, replica_groups=mesh['x'=4,'za'=2,'zb'=4,'y'=4,'zh'=2,'c'=2] {'x','y'}, dimensions={0} | all-to-all | bytes 2097152 | tf_op jit(solution)/shard_map/gradient_exchange/all_to_all | solution.py:49
  112.9 4.1 %fusion = bf16[256,1280]{1,0:T(8,128)(2,1)S(1)} fusion(bf16[16,256,128]{2,1,0:T(8,128)(2,1)S(1)} %all_to_all.30, bf16[16,128,1280]{2,1,0:T(8,128)(2,1)} %all-to-all-done.after_ref), kind=kOutput, calls=%fused_computation.1 | convolution fusion | flops 1342504960 | bytes 6946816 | tf_op jit(solution)/shard_map/projection/bcr,brf->cf/dot_general | solution.py:242
  117.0 7.6 %all_to_all.31 = bf16[2,128,1280]{2,1,0:T(8,128)(2,1)S(1)} all-to-all(bf16[2,128,1280]{2,1,0:T(8,128)(2,1)S(1)} %bitcast.31), channel_id=1, replica_groups=mesh['x'=4,'za'=2,'zb'=4,'y'=4,'zh'=2,'c'=2] {'c'}, dimensions={0} | all-to-all | bytes 1310720 | tf_op jit(solution)/shard_map/core_sum/all_to_all | solution.py:49
  124.6 0.1 reduce_sum.36
  124.7 0.2 copy.16
  125.0 21.2 %all_to_all.32 = bf16[4,2,160,128]{3,2,1,0:T(8,128)(2,1)S(1)} all-to-all(bf16[4,2,160,128]{3,2,1,0:T(8,128)(2,1)S(1)} %copy.17), channel_id=1, replica_groups=mesh['x'=4,'za'=2,'zb'=4,'y'=4,'zh'=2,'c'=2] {'zb'}, dimensions={0} | all-to-all | bytes 655360 | tf_op jit(solution)/shard_map/z_sum/all_to_all | solution.py:49
  146.2 25.8 %all_to_all.33 = bf16[4,160,128]{2,1,0:T(8,128)(2,1)S(1)} all-to-all(bf16[4,160,128]{2,1,0:T(8,128)(2,1)S(1)} %bitcast.32), channel_id=1, replica_groups=mesh['x'=4,'za'=2,'zb'=4,'y'=4,'zh'=2,'c'=2] {'zh','za'}, dimensions={0} | all-to-all | bytes 327680 | tf_op jit(solution)/shard_map/z_sum/all_to_all | solution.py:49
  172.1 12.9 %all_to_all.34 = bf16[8,160,128]{2,1,0:T(8,128)(2,1)S(1)} all-to-all(bf16[8,160,128]{2,1,0:T(8,128)(2,1)S(1)} %broadcast_in_dim.5), channel_id=1, replica_groups=mesh['x'=4,'za'=2,'zb'=4,'y'=4,'zh'=2,'c'=2] {'y','c'}, dimensions={0} | all-to-all | bytes 655360 | tf_op jit(solution)/shard_map/replicate/all_to_all | solution.py:49
  185.1 0.2 copy.19
  185.3 0.2 copy.18
  185.5 0.9 copy_bitcast_fusion
  (7 shorter events, 0.3 us)
Async XLA Ops:
  4.4 85.6 %all-to-all-start = ((bf16[16,128,1280]{2,1,0:T(8,128)(2,1)}), bf16[16,128,1280]{2,1,0:T(8,128)(2,1)}, u32[]{:S(2)}, u32[]{:S(2)}) async-start(bf16[16,128,1280]{2,1,0:T(8,128)(2,1)} %feature_blocks.1), calls=%async_computation | async-start | bytes 10485760 | tf_op jit(solution)/shard_map/inputs_exchange/all_to_all | solution.py:49
  13.8 31.6 %collective-permute-start.1 = (bf16[272,512]{1,0:T(8,128)(2,1)}, bf16[272,512]{1,0:T(8,128)(2,1)S(1)}, u32[]{:S(2)}, u32[]{:S(2)}) collective-permute-start(bf16[272,512]{1,0:T(8,128)(2,1)} %packed_tile.1), channel_id=1, source_target_pairs={{480,0},{496,16},{0,32},{16,48},{32,64},{48,80},{64,96},{80,112},{... | collective-permute-start | bytes 835592 | tf_op jit(solution)/shard_map/keys_values_halo/ppermute | solution.py:30
  18.7 26.8 %collective-permute-start = (bf16[272,512]{1,0:T(8,128)(2,1)}, bf16[272,512]{1,0:T(8,128)(2,1)S(1)}, u32[]{:S(2)}, u32[]{:S(2)}) collective-permute-start(bf16[272,512]{1,0:T(8,128)(2,1)} %packed_tile.1), channel_id=1, source_target_pairs={{496,0},{0,16},{16,32},{32,48},{48,64},{64,80},{80,96},{96,112},{1... | collective-permute-start | bytes 835592 | tf_op jit(solution)/shard_map/keys_values_halo/ppermute | solution.py:30
  22.2 30.5 %collective-permute-start.2 = (bf16[272,512]{1,0:T(8,128)(2,1)}, bf16[272,512]{1,0:T(8,128)(2,1)S(1)}, u32[]{:S(2)}, u32[]{:S(2)}) collective-permute-start(bf16[272,512]{1,0:T(8,128)(2,1)} %packed_tile.1), channel_id=1, source_target_pairs={{80,128},{208,256},{336,384},{464,0},{81,129},{209,257},{337,385},... | collective-permute-start | bytes 835592 | tf_op jit(solution)/shard_map/keys_values_halo/ppermute | solution.py:35
  45.4 8.1 %copy-start.3 = (bf16[272,512]{1,0:T(8,128)(2,1)}, bf16[272,512]{1,0:T(8,128)(2,1)S(1)}, u32[]{:S(2)}) copy-start(bf16[272,512]{1,0:T(8,128)(2,1)S(1)} %collective-permute-done.1.t2_ref) | copy-start | bytes 835588
  45.4 8.1 %copy-start.4 = (bf16[272,512]{1,0:T(8,128)(2,1)}, bf16[272,512]{1,0:T(8,128)(2,1)S(1)}, u32[]{:S(2)}) copy-start(bf16[272,512]{1,0:T(8,128)(2,1)S(1)} %collective-permute-done.t1_ref) | copy-start | bytes 835588
  45.4 7.3 %collective-permute-start.3 = (bf16[272,512]{1,0:T(8,128)(2,1)S(1)}, bf16[272,512]{1,0:T(8,128)(2,1)S(1)}, u32[]{:S(2)}, u32[]{:S(2)}) collective-permute-start(bf16[272,512]{1,0:T(8,128)(2,1)S(1)} %collective-permute-done.1.t2_ref), channel_id=1, source_target_pairs={{0,16},{16,32},{32,48},{48,64},{64,80},{80,96},{96,112},{1,17},{17... | collective-permute-start | bytes 835592 | tf_op jit(solution)/shard_map/keys_values_halo/ppermute | solution.py:36
  61.9 13.0 %collective-permute-start.5 = (bf16[2,2,128,256]{3,2,1,0:T(8,128)(2,1)}, bf16[2,2,128,256]{3,2,1,0:T(8,128)(2,1)S(1)}, u32[]{:S(2)}, u32[]{:S(2)}) collective-permute-start(bf16[2,2,128,256]{3,2,1,0:T(8,128)(2,1)} %get-tuple-element.14), channel_id=1, source_target_pairs={{16,0},{32,16},{48,32},{64,48},{80,64},{96,80},{112,96},{17,1},{33... | collective-permute-start | bytes 786440 | tf_op jit(solution)/shard_map/gradient_return/ppermute | solution.py:42
  63.2 19.9 %collective-permute-start.7 = (bf16[2,2,128,256]{3,2,1,0:T(8,128)(2,1)}, bf16[2,2,128,256]{3,2,1,0:T(8,128)(2,1)S(1)}, u32[]{:S(2)}, u32[]{:S(2)}) collective-permute-start(bf16[2,2,128,256]{3,2,1,0:T(8,128)(2,1)} %get-tuple-element.14), channel_id=1, source_target_pairs={{0,464},{128,80},{256,208},{384,336},{1,465},{129,81},{257,209},{3... | collective-permute-start | bytes 786440 | tf_op jit(solution)/shard_map/gradient_return/ppermute | solution.py:43
  72.9 10.1 %collective-permute-start.4 = (bf16[2,2,128,256]{3,2,1,0:T(8,128)(2,1)}, bf16[2,2,128,256]{3,2,1,0:T(8,128)(2,1)S(1)}, u32[]{:S(2)}, u32[]{:S(2)}) collective-permute-start(bf16[2,2,128,256]{3,2,1,0:T(8,128)(2,1)} %get-tuple-element.12), channel_id=1, source_target_pairs={{16,0},{32,16},{48,32},{64,48},{80,64},{96,80},{112,96},{128,112},... | collective-permute-start | bytes 786440 | tf_op jit(solution)/shard_map/gradient_return/ppermute | solution.py:30
  75.9 14.1 %collective-permute-start.6 = (bf16[2,2,128,256]{3,2,1,0:T(8,128)(2,1)S(1)}, bf16[2,2,128,256]{3,2,1,0:T(8,128)(2,1)S(1)}, u32[]{:S(2)}, u32[]{:S(2)}) collective-permute-start(bf16[2,2,128,256]{3,2,1,0:T(8,128)(2,1)S(1)} %add_convert_fusion), channel_id=1, source_target_pairs={{32,0},{48,16},{64,32},{80,48},{96,64},{112,80},{128,96},{144,112}... | collective-permute-start | bytes 786440 | tf_op jit(solution)/shard_map/gradient_return/ppermute | solution.py:30
  83.1 7.0 %copy-start.1 = (bf16[2,2,128,256]{3,2,1,0:T(8,128)(2,1)}, bf16[2,2,128,256]{3,2,1,0:T(8,128)(2,1)S(1)}, u32[]{:S(2)}) copy-start(bf16[2,2,128,256]{3,2,1,0:T(8,128)(2,1)S(1)} %collective-permute-done.4.b1_ref) | copy-start | bytes 786436
  83.1 7.0 %copy-start = (bf16[2,2,128,256]{3,2,1,0:T(8,128)(2,1)}, bf16[2,2,128,256]{3,2,1,0:T(8,128)(2,1)S(1)}, u32[]{:S(2)}) copy-start(bf16[2,2,128,256]{3,2,1,0:T(8,128)(2,1)S(1)} %collective-permute-done.7.b3_ref) | copy-start | bytes 786436
  90.0 0.7 copy-start.2

commit v4 on v3

--- a/solution.py
+++ b/solution.py
@@ -16,6 +16,7 @@
 HALF = ROWS // 2
 WINDOW = 4
 DOCUMENTS = 8
+PER_STEP = 4
 SCALE = HEAD ** (-0.5)
 LINE = ("za", "zb")
 CTX = ("x",) + LINE
@@ -34,7 +35,7 @@
     nx, nz = lax.axis_size("x"), lax.axis_size(LINE)
     across = lax.ppermute(block, CTX, [(x * nz + nz - 3, (x + 1) % nx * nz) for x in range(nx)])
     along = lax.ppermute(second, LINE, [(z, z + 1) for z in range(nz - 1)])
-    return jnp.where(lax.axis_index(LINE) == 0, across, along)
+    return along, across
 
 
 def returned(first, second, third):
@@ -45,6 +46,29 @@
     return shifted(first, -1), shifted(second, -2), across
 
 
+def neighbours(block, axis):
+    n = lax.axis_size(axis)
+    return tuple(lax.ppermute(block, axis, [(i, (i + by) % n) for i in range(n)]) for by in (1, -1))
+
+
+def opposite(before, after, axis):
+    return neighbours(before, axis)[0], neighbours(after, axis)[1]
+
+
+def settled(first, second):
+    anywhere = pl.BlockSpec(memory_space=pl.ANY)
+    return pl.pallas_call(
+        lambda *refs: None,
+        in_specs=[anywhere] * 2,
+        out_specs=[anywhere] * 2,
+        out_shape=[jax.ShapeDtypeStruct(a.shape, a.dtype) for a in (first, second)],
+        input_output_aliases={0: 0, 1: 1},
+        compiler_params=pltpu.CompilerParams(vmem_limit_bytes=VMEM_LIMIT),
+        cost_estimate=pl.CostEstimate(flops=30000000000, bytes_accessed=0, transcendentals=0),
+        name="settled",
+    )(first, second)
+
+
 def exchange(blocks, axes):
     return lax.all_to_all(blocks, axes, 0, 0, tiled=True)
 
@@ -54,10 +78,10 @@
 
 
 def attention_kernel(
-    span_ref, seg_ref, q_ref, g_ref, k_ref, v_ref, t1_ref, t2_ref, t3_ref,
+    span_ref, seg_ref, q_ref, g_ref, k_ref, v_ref, t1_ref, t2_ref, along_ref, across_ref,
     dq_ref, own_ref, r1_ref, r2_ref, r3_ref, bias_ref,
 ):
-    tiles = (t1_ref, t2_ref, t3_ref)
+    placed = {1: (t1_ref,), 2: (t2_ref,), 3: (along_ref, across_ref)}
 
     @pl.when(pl.program_id(0) == 0)
     def _():
@@ -75,35 +99,47 @@
                     span = span_ref[half]
                 else:
                     at = 2 * ROWS + 8 * half
-                    span = tiles[step - 1][at : at + 8, :].astype(F32)[0:1, :].astype(jnp.int32)
+                    span = sum(t[at : at + 8, 0:ROWS].astype(F32) for t in placed[step])
+                    span = span[0:1, :].astype(jnp.int32)
                 pos_k = span * HALF + row
                 allowed = (pos_k <= pos_q) & (pos_k >= start)
                 at = step * ROWS + half * HALF
                 bias_ref[at : at + HALF, :] = jnp.where(allowed, 0.0, -1e30)
 
-    k = jnp.concatenate([k_ref[...]] + [t[0:ROWS, :] for t in tiles], axis=0)
-    v = jnp.concatenate([v_ref[...]] + [t[ROWS : 2 * ROWS, :] for t in tiles], axis=0)
-    heads = [slice(c * HEAD, (c + 1) * HEAD) for c in range(SHARING)]
-    q = jnp.concatenate([q_ref[:, h] for h in heads], axis=0)
-    g = jnp.concatenate([g_ref[:, h] for h in heads], axis=0)
-    bias = bias_ref[...]
-    s = dot(k, q, 1, 1) + jnp.concatenate([bias] * SHARING, axis=1)
-    e = jnp.exp2((s - jnp.max(s, axis=0, keepdims=True)) * (SCALE * math.log2(math.e)))
-    p = e * (1.0 / jnp.sum(e, axis=0, keepdims=True))
-    dp = dot(v, g, 1, 1)
-    delta = jnp.sum(p * dp, axis=0, keepdims=True)
-    ds = (p * (dp - delta)).astype(BF16)
-    dv = dot(p.astype(BF16), g, 1, 0)
-    dk = dot(ds, q, 1, 0) * SCALE
-    dq = (dot(ds, k, 0, 0) * SCALE).astype(BF16)
-    for c, h in enumerate(heads):
-        dq_ref[:, h] = dq[c * ROWS : (c + 1) * ROWS, :]
-    own_ref[0] = dk[0:ROWS]
-    own_ref[1] = dv[0:ROWS]
-    for step, ref in enumerate((r1_ref, r2_ref, r3_ref), 1):
-        rows = slice(step * ROWS, (step + 1) * ROWS)
-        ref[0] = dk[rows].astype(BF16)
-        ref[1] = dv[rows].astype(BF16)
+    for head in range(q_ref.shape[1] // (SHARING * HEAD)):
+        own = slice(head * HEAD, (head + 1) * HEAD)
+        k, v = (
+            jnp.concatenate(
+                [first[:, own], t1_ref[rows, own], t2_ref[rows, own]]
+                + [along_ref[rows, own] + across_ref[rows, own]],
+                axis=0,
+            )
+            for first, rows in ((k_ref, slice(0, ROWS)), (v_ref, slice(ROWS, 2 * ROWS)))
+        )
+        heads = [
+            slice(c * HEAD, (c + 1) * HEAD) for c in range(head * SHARING, (head + 1) * SHARING)
+        ]
+        q = jnp.concatenate([q_ref[:, h] for h in heads], axis=0)
+        g = jnp.concatenate([g_ref[:, h] for h in heads], axis=0)
+        bias = bias_ref[...]
+        s = dot(k, q, 1, 1) + jnp.concatenate([bias] * SHARING, axis=1)
+        e = jnp.exp2((s - jnp.max(s, axis=0, keepdims=True)) * (SCALE * math.log2(math.e)))
+        p = e * (1.0 / jnp.sum(e, axis=0, keepdims=True))
+        dp = dot(v, g, 1, 1)
+        delta = jnp.sum(p * dp, axis=0, keepdims=True)
+        ds = (p * (dp - delta)).astype(BF16)
+        dv = dot(p.astype(BF16), g, 1, 0)
+        dk = dot(ds, q, 1, 0) * SCALE
+        dq = (dot(k, ds, 0, 0) * SCALE).T.astype(BF16)
+        for c, h in enumerate(heads):
+            dq_ref[:, h] = dq[c * ROWS : (c + 1) * ROWS, :]
+        pair, at = head // 2, slice(head % 2 * HEAD, (head % 2 + 1) * HEAD)
+        own_ref[0, pair, :, at] = dk[0:ROWS]
+        own_ref[1, pair, :, at] = dv[0:ROWS]
+        for step, ref in enumerate((r1_ref, r2_ref, r3_ref), 1):
+            rows = slice(step * ROWS, (step + 1) * ROWS)
+            ref[0, pair, :, at] = dk[rows].astype(BF16)
+            ref[1, pair, :, at] = dv[rows].astype(BF16)
 
 
 def tile_kernel(span_ref, k_ref, v_ref, tile_ref):
@@ -159,47 +195,47 @@
     )(inputs)
 
 
-def sum_kernel(own_ref, b1_ref, b2_ref, b3_ref, after_ref, out_ref):
-    del after_ref
+def sum_kernel(own_ref, b1_ref, b2_ref, b3_ref, *refs):
+    out_ref = refs[-1]
     total = own_ref[...]
     for ref in (b1_ref, b2_ref, b3_ref):
         total = total + ref[...].astype(F32)
     for i in range(2):
         for j in range(2):
             turned = total[i, j].T.astype(BF16)
-            for copy in range(out_ref.shape[0]):
-                out_ref[copy, 2 * i + j] = turned
+            for copy in range(out_ref.shape[1]):
+                out_ref[2 * i + j, copy] = turned
 
 
 def sum_terms(own, back, copies, after):
     whole = pl.BlockSpec(memory_space=pltpu.VMEM)
     return pl.pallas_call(
         sum_kernel,
-        in_specs=[whole] * 4 + [pl.BlockSpec(memory_space=pl.ANY)],
+        in_specs=[whole] * 4 + [pl.BlockSpec(memory_space=pl.ANY)] * len(after),
         out_specs=whole,
-        out_shape=jax.ShapeDtypeStruct((copies, 4, own.shape[3], own.shape[2]), BF16),
+        out_shape=jax.ShapeDtypeStruct((4, copies, own.shape[3], own.shape[2]), BF16),
         compiler_params=pltpu.CompilerParams(vmem_limit_bytes=VMEM_LIMIT),
         cost_estimate=pl.CostEstimate(
-            flops=own.size * 4, bytes_accessed=own.size * 18, transcendentals=0
+            flops=20000000000, bytes_accessed=own.size * 18, transcendentals=0
         ),
         name="sum_terms",
-    )(own, *back, after)
+    )(own, *back, *after)
 
 
 def attention(span, segments, queries, gradient, keys, values, tiles):
-    wide = pl.BlockSpec((None, ROWS, SHARING * HEAD), lambda i: (0, 0, i))
-    narrow = pl.BlockSpec((None, ROWS, HEAD), lambda i: (0, 0, i))
-    tile = pl.BlockSpec((tiles[0].shape[0], HEAD), lambda i: (0, i))
-    term = pl.BlockSpec((2, None, ROWS, HEAD), lambda i: (0, i // 2, 0, i % 2))
+    wide = pl.BlockSpec((None, ROWS, PER_STEP * SHARING * HEAD), lambda i: (0, 0, i))
+    narrow = pl.BlockSpec((None, ROWS, PER_STEP * HEAD), lambda i: (0, 0, i))
+    tile = pl.BlockSpec((tiles[0].shape[0], PER_STEP * HEAD), lambda i: (0, i))
+    term = pl.BlockSpec((2, PER_STEP // 2, ROWS, 2 * HEAD), lambda i: (0, i, 0, 0))
     terms = (2, 2, ROWS, 2 * HEAD)
     work = QUERY_HEADS * ROWS * WINDOW * ROWS
     return pl.pallas_call(
         attention_kernel,
-        grid=(KEY_VALUE_HEADS,),
+        grid=(KEY_VALUE_HEADS // PER_STEP,),
         in_specs=[
             pl.BlockSpec(memory_space=pltpu.SMEM),
             pl.BlockSpec(segments.shape, lambda i: (0, 0)),
-            wide, wide, narrow, narrow, tile, tile, tile,
+            wide, wide, narrow, narrow, tile, tile, tile, tile,
         ],
         out_specs=[wide, term, term, term, term],
         out_shape=[
@@ -210,9 +246,9 @@
             jax.ShapeDtypeStruct(terms, BF16),
         ],
         scratch_shapes=[pltpu.VMEM((WINDOW * ROWS, ROWS), F32)],
-        compiler_params=pltpu.CompilerParams(vmem_limit_bytes=VMEM_LIMIT),
+        compiler_params=pltpu.CompilerParams(vmem_limit_bytes=24 * 1024 * 1024),
         cost_estimate=pl.CostEstimate(
-            flops=10 * HEAD * work, bytes_accessed=5 * 1024 * 1024, transcendentals=work
+            flops=60 * HEAD * work, bytes_accessed=5 * 1024 * 1024, transcendentals=work
         ),
         name="attention",
     )(span, segments, queries, gradient, keys, values, *tiles)
@@ -225,21 +261,33 @@
     with jax.named_scope("keys_values_halo"):
         tile = packed_tile(span_ids, keys, values)
         tiles = [shifted(tile, 1), shifted(tile, 2)]
-        tiles.append(beyond(tile, lax.optimization_barrier((tiles[1], tiles[0]))[0]))
+        tiles.extend(beyond(tile, lax.optimization_barrier((tiles[1], tiles[0]))[0]))
     with jax.named_scope("inputs_exchange"):
-        blocks = feature_blocks(inputs, nx, ny)
-        features_x = exchange(blocks, ("x", "y"))
+        held = exchange(feature_blocks(inputs, nx, 1), ("x",))
+        held, *_ = lax.optimization_barrier((held, *tiles[:2]))
+        before, after = neighbours(held, "y")
     with jax.named_scope("attention"):
         grad_queries, own, *terms = attention(
             span_ids, segments, queries, output_gradient, keys, values, tiles
         )
     with jax.named_scope("gradient_return"):
         back = returned(*terms)
-        blocks = sum_terms(own, back, nx, features_x)
+        halves = before[: nx // 2], after[nx // 2 :]
+        blocks = sum_terms(own, back, nx, halves)
     with jax.named_scope("gradient_exchange"):
-        columns = exchange(blocks.reshape(nx * ny, 2 * HEAD, rows), ("x", "y"))
+        columns = exchange(blocks.reshape(ny * nx, 2 * HEAD, rows), ("y", "x"))
     with jax.named_scope("projection"):
-        partial = jnp.einsum("bcr,brf->cf", columns, features_x, preferred_element_type=F32)
+        me = lax.axis_index("y")
+        columns = columns.reshape(ny, nx, 2 * HEAD, rows)
+        across_y = settled(*opposite(*halves, "y"))
+        columns, *across_y = lax.optimization_barrier((columns, *across_y))
+        features_x = held, after, across_y, before
+        partial = jnp.zeros((2 * HEAD, part), F32)
+        for step in (0, 1, 3, 2):
+            blocks = features_x[step]
+            match = lax.dynamic_index_in_dim(columns, (me + step) % ny, 0, keepdims=False)
+            blocks = jnp.concatenate(blocks, axis=0) if step == 2 else blocks
+            partial += jnp.einsum("bcr,brf->cf", match, blocks, preferred_element_type=F32)
     with jax.named_scope("core_sum"):
         halves = exchange(partial.astype(BF16).reshape(nc, HEAD, part), ("c",))
         pair = jnp.sum(halves.astype(F32), axis=0).astype(BF16)

time: 187 us -> 182 us (0.973)
  blocking collectives: 87.1 us -> 60 us
  waiting for transfers between devices: 37.9 us -> 52.4 us
  starting transfers between devices: 35.7 us -> 41.7 us
  Pallas kernels: 16.3 us -> 13 us
  matrix products: 4.07 us -> 7.15 us
  local copies, waits for them, and re-layouts: 2.35 us -> 4.78 us
    all_to_all x5 -> x4, blocking collectives: 87.1 us -> 60 us  [exchange(): return lax.all_to_all(blocks, axes, 0, 0, tiled=True)]
    ppermute x0 -> x4, waiting for transfers between devices: none -> 23.8 us  [neighbours(): lax.ppermute(block, axis, [(i, (i + by) % n) for i in range(n)])]
    ppermute x0 -> x4, starting transfers between devices: none -> 13.1 us  [neighbours(): lax.ppermute(block, axis, [(i, (i + by) % n) for i in range(n)])]
    ppermute x4, waiting for transfers between devices: 31.9 us -> 24.8 us  [shifted(): return lax.ppermute(block, CTX, [((i - distance) % n, i) for i in range(n)])]
    ppermute x1, starting transfers between devices: 9.75 us -> 2.83 us  [returned(): lax.ppermute(third, CTX, [(x * nz, (x - 1) % nx * nz + nz - 3) for x in r...]
    ppermute x1, waiting for transfers between devices: 6.02 us -> 0.01 us  [beyond(): lax.ppermute(block, CTX, [(x * nz + nz - 3, (x + 1) % nx * nz) for x in r...]
    dot_general x1 -> x4, matrix products: 4.07 us -> 7.15 us  [on_device(): jnp.einsum('bcr,brf->cf', match, blocks, preferred_element_type=F32)]
    slice x0 -> x2, local copies, waits for them, and re-layouts: none -> 2.26 us  [on_device(): halves = (before[:nx // 2], after[nx // 2:])]
  transfers between devices with their start and end apart: 9 -> 14, of which waited for: 4 -> 7; matrix products, arithmetic and copies ran while one was open for 1% -> 1% of each run, Pallas kernels for 5% -> 6%
where the time goes in v4:
time: 182 us; the launch traced here: 181 us
  blocking collectives  60 us (33%)
  waiting for transfers between devices  52.4 us (29%)
  starting transfers between devices  41.7 us (23%)
  Pallas kernels  13 us (7%)
  matrix products  7.15 us (4%)
  local copies, waits for them, and re-layouts  4.78 us (3%)
    all_to_all x4, blocking collectives, exchange(): return lax.all_to_all(blocks, axes, 0, 0, tiled=True)  60 us
    ppermute x4, waiting for transfers between devices, shifted(): return lax.ppermute(block, CTX, [((i - distance) % n, i) for i in range(n)])  24.8 us
    ppermute x4, waiting for transfers between devices, neighbours(): lax.ppermute(block, axis, [(i, (i + by) % n) for i in range(n)])  23.8 us
    ppermute x4, starting transfers between devices, shifted(): return lax.ppermute(block, CTX, [((i - distance) % n, i) for i in range(n)])  13.3 us
    ppermute x4, starting transfers between devices, neighbours(): lax.ppermute(block, axis, [(i, (i + by) % n) for i in range(n)])  13.1 us
    all_to_all x2, starting transfers between devices, exchange(): return lax.all_to_all(blocks, axes, 0, 0, tiled=True)  8.64 us
    dot_general x4, matrix products, on_device(): jnp.einsum('bcr,brf->cf', match, blocks, preferred_element_type=F32)  7.15 us
    pallas_call x1, Pallas kernels, attention(): pl.pallas_call(attention_kernel, grid=(KEY_VALUE_HEADS // PER_STEP,), in_...  6.46 us
  transfers between devices with their start and end apart: 14, of which 7 were waited for; matrix products, arithmetic and copies ran while one was open for 1% of the time, Pallas kernels for 6%

profile of v4, /device:TPU:1, one launch (start us, length us, event | category | flops | bytes accessed | tf_op | source)
XLA Modules:
  0.0 180.6 jit_solution(295010371988281488)
XLA Ops:
  0.6 2.4 %feature_blocks.1 = bf16[4,128,1280]{2,1,0:T(8,128)(2,1)} custom-call(bf16[1,128,5120]{2,1,0:T(8,128)(2,1)} %x_ref.1), custom_call_target="tpu_custom_call" | custom-call | bytes 2621440 | tf_op jit(solution)/shard_map/inputs_exchange/feature_blocks/pallas_call | solution.py:184
  3.1 0.0 copy-start
  3.1 0.0 copy-start.1
  3.1 0.0 copy-start.4
  3.1 0.0 copy-start.5
  3.1 5.0 %all-to-all-start = ((bf16[4,128,1280]{2,1,0:T(8,128)(2,1)}), bf16[4,128,1280]{2,1,0:T(8,128)(2,1)}, u32[]{:S(2)}, u32[]{:S(2)}) async-start(bf16[4,128,1280]{2,1,0:T(8,128)(2,1)} %feature_blocks.1), calls=%async_computation | async-start | bytes 2621440 | tf_op jit(solution)/shard_map/inputs_exchange/all_to_all | solution.py:73
  8.1 1.7 packed_tile.1
  9.8 3.8 %collective-permute-start = (bf16[272,512]{1,0:T(8,128)(2,1)}, bf16[272,512]{1,0:T(8,128)(2,1)S(1)}, u32[]{:S(2)}, u32[]{:S(2)}) collective-permute-start(bf16[272,512]{1,0:T(8,128)(2,1)} %packed_tile.1), channel_id=1, source_target_pairs={{496,0},{0,16},{16,32},{32,48},{48,64},{64,80},{80,96},{96,112},{1... | collective-permute-start | bytes 835592 | tf_op jit(solution)/shard_map/keys_values_halo/ppermute | solution.py:31
  13.7 4.9 %collective-permute-start.1 = (bf16[272,512]{1,0:T(8,128)(2,1)}, bf16[272,512]{1,0:T(8,128)(2,1)S(1)}, u32[]{:S(2)}, u32[]{:S(2)}) collective-permute-start(bf16[272,512]{1,0:T(8,128)(2,1)} %packed_tile.1), channel_id=1, source_target_pairs={{480,0},{496,16},{0,32},{16,48},{32,64},{48,80},{64,96},{80,112},{... | collective-permute-start | bytes 835592 | tf_op jit(solution)/shard_map/keys_values_halo/ppermute | solution.py:31
  18.6 1.3 collective-permute-start.3
  19.9 9.7 %collective-permute-done.t1_ref = bf16[272,512]{1,0:T(8,128)(2,1)S(1)} collective-permute-done((bf16[272,512]{1,0:T(8,128)(2,1)}, bf16[272,512]{1,0:T(8,128)(2,1)S(1)}, u32[]{:S(2)}, u32[]{:S(2)}) %collective-permute-start) | collective-permute-done | bytes 278560 | tf_op jit(solution)/shard_map/keys_values_halo/ppermute | solution.py:31
  29.5 15.1 %collective-permute-done.1.t2_ref = bf16[272,512]{1,0:T(8,128)(2,1)S(1)} collective-permute-done((bf16[272,512]{1,0:T(8,128)(2,1)}, bf16[272,512]{1,0:T(8,128)(2,1)S(1)}, u32[]{:S(2)}, u32[]{:S(2)}) %collective-permute-start.1) | collective-permute-done | bytes 278560 | tf_op jit(solution)/shard_map/keys_values_halo/ppermute | solution.py:31
  44.6 1.3 collective-permute-start.2
  45.9 3.2 %collective-permute-start.8 = (bf16[4,128,1280]{2,1,0:T(8,128)(2,1)}, bf16[4,128,1280]{2,1,0:T(8,128)(2,1)}, u32[]{:S(2)}, u32[]{:S(2)}) collective-permute-start(bf16[4,128,1280]{2,1,0:T(8,128)(2,1)} %all-to-all-done), channel_id=1, source_target_pairs={{0,4},{4,8},{8,12},{12,0},{1,5},{5,9},{9,13},{13,1},{2,6},{6,10},{... | collective-permute-start | bytes 3932168 | tf_op jit(solution)/shard_map/inputs_exchange/ppermute | solution.py:51
  49.2 3.4 %collective-permute-start.9 = (bf16[4,128,1280]{2,1,0:T(8,128)(2,1)}, bf16[4,128,1280]{2,1,0:T(8,128)(2,1)}, u32[]{:S(2)}, u32[]{:S(2)}) collective-permute-start(bf16[4,128,1280]{2,1,0:T(8,128)(2,1)} %all-to-all-done), channel_id=1, source_target_pairs={{0,12},{4,0},{8,4},{12,8},{1,13},{5,1},{9,5},{13,9},{2,14},{6,2},{... | collective-permute-start | bytes 3932168 | tf_op jit(solution)/shard_map/inputs_exchange/ppermute | solution.py:51
  52.6 6.5 %attention.1 = (bf16[1,128,2560]{2,1,0:T(8,128)(2,1)}, f32[2,2,128,256]{3,2,1,0:T(8,128)S(1)}, bf16[2,2,128,256]{3,2,1,0:T(8,128)(2,1)S(1)}, bf16[2,2,128,256]{3...) custom-call(s32[2]{0:T(128)S(1)} %copy-done.2, s32[1,4096]{1,0:T(1,128)S(1)} %copy-done.5, ...), custom_call_target="tpu_custom_call" | custom-call | flops 10066329600 | bytes 5242880 | tf_op jit(solution)/shard_map/attention/attention/pallas_call | solution.py:232
  59.1 1.3 collective-permute-start.5
  60.4 2.8 %collective-permute-start.7 = (bf16[2,2,128,256]{3,2,1,0:T(8,128)(2,1)S(1)}, bf16[2,2,128,256]{3,2,1,0:T(8,128)(2,1)S(1)}, u32[]{:S(2)}, u32[]{:S(2)}) collective-permute-start(bf16[2,2,128,256]{3,2,1,0:T(8,128)(2,1)S(1)} %get-tuple-element.20), channel_id=1, source_target_pairs={{0,464},{128,80},{256,208},{384,336},{1,465},{129,81},{257,209},{3... | collective-permute-start | bytes 786440 | tf_op jit(solution)/shard_map/gradient_return/ppermute | solution.py:44
  63.2 2.6 %collective-permute-start.4 = (bf16[2,2,128,256]{3,2,1,0:T(8,128)(2,1)S(1)}, bf16[2,2,128,256]{3,2,1,0:T(8,128)(2,1)S(1)}, u32[]{:S(2)}, u32[]{:S(2)}) collective-permute-start(bf16[2,2,128,256]{3,2,1,0:T(8,128)(2,1)S(1)} %get-tuple-element.18), channel_id=1, source_target_pairs={{16,0},{32,16},{48,32},{64,48},{80,64},{96,80},{112,96},{128,112},... | collective-permute-start | bytes 786440 | tf_op jit(solution)/shard_map/gradient_return/ppermute | solution.py:31
  65.8 2.0 %collective-permute-done.5 = bf16[2,2,128,256]{3,2,1,0:T(8,128)(2,1)S(1)} collective-permute-done((bf16[2,2,128,256]{3,2,1,0:T(8,128)(2,1)S(1)}, bf16[2,2,128,256]{3,2,1,0:T(8,128)(2,1)S(1)}, u32[]{:S(2)}, u32[]{:S(2)}) %collective-permute-start.5) | collective-permute-done | bytes 262176 | tf_op jit(solution)/shard_map/gradient_return/ppermute | solution.py:43
  67.8 0.1 add_convert_fusion
  67.9 2.0 %collective-permute-start.6 = (bf16[2,2,128,256]{3,2,1,0:T(8,128)(2,1)S(1)}, bf16[2,2,128,256]{3,2,1,0:T(8,128)(2,1)S(1)}, u32[]{:S(2)}, u32[]{:S(2)}) collective-permute-start(bf16[2,2,128,256]{3,2,1,0:T(8,128)(2,1)S(1)} %add_convert_fusion), channel_id=1, source_target_pairs={{32,0},{48,16},{64,32},{80,48},{96,64},{112,80},{128,96},{144,112}... | collective-permute-start | bytes 786440 | tf_op jit(solution)/shard_map/gradient_return/ppermute | solution.py:31
  69.9 9.4 %collective-permute-done.8 = bf16[4,128,1280]{2,1,0:T(8,128)(2,1)} collective-permute-done((bf16[4,128,1280]{2,1,0:T(8,128)(2,1)}, bf16[4,128,1280]{2,1,0:T(8,128)(2,1)}, u32[]{:S(2)}, u32[]{:S(2)}) %collective-permute-start.8) | collective-permute-done | bytes 1310752 | tf_op jit(solution)/shard_map/inputs_exchange/ppermute | solution.py:51
  79.3 1.1 slice.18.refs_0_
  80.4 1.9 %collective-permute-start.10 = (bf16[2,128,1280]{2,1,0:T(8,128)(2,1)S(1)}, bf16[2,128,1280]{2,1,0:T(8,128)(2,1)S(1)}, u32[]{:S(2)}, u32[]{:S(2)}) collective-permute-start(bf16[2,128,1280]{2,1,0:T(8,128)(2,1)S(1)} %slice.18.refs_0_), channel_id=1, source_target_pairs={{0,4},{4,8},{8,12},{12,0},{1,5},{5,9},{9,13},{13,1},{2,6},{6,10},{... | collective-permute-start | bytes 1966088 | tf_op jit(solution)/shard_map/projection/ppermute | solution.py:51
  82.4 1.1 slice.19.refs_1_
  83.5 4.6 %collective-permute-start.11 = (bf16[2,128,1280]{2,1,0:T(8,128)(2,1)S(1)}, bf16[2,128,1280]{2,1,0:T(8,128)(2,1)}, u32[]{:S(2)}, u32[]{:S(2)}) collective-permute-start(bf16[2,128,1280]{2,1,0:T(8,128)(2,1)S(1)} %slice.19.refs_1_), channel_id=1, source_target_pairs={{0,12},{4,0},{8,4},{12,8},{1,13},{5,1},{9,5},{13,9},{2,14},{6,2},{... | collective-permute-start | bytes 1966088 | tf_op jit(solution)/shard_map/projection/ppermute | solution.py:51
  88.2 0.6 copy-done.12
  88.8 0.1 copy-done.11
  88.9 0.1 copy-done.13
  89.0 2.4 %sum_terms.1 = bf16[4,4,256,128]{3,2,1,0:T(8,128)(2,1)} custom-call(f32[2,2,128,256]{3,2,1,0:T(8,128)} %copy-done.6, bf16[2,2,128,256]{3,2,1,0:T(8,128)(2,1)} %copy-done.12, bf16[2,2,128,256]{3,2,1,0:T(8,128)(2,1)} %copy-done.13, bf16[2,2,128,256]{3,2,1,0:T(8,128)(2,1)} %copy-done.11, bf16[2,128,1280]{2,1,0:T(8,128)(2,1)} %copy-done.7, ...), custom_call_target="tpu_custom_call" | custom-call | flops 20000000000 | bytes 2359296 | tf_op jit(solution)/shard_map/gradient_return/sum_terms/pallas_call | solution.py:212
  91.4 3.7 %all-to-all-start.1 = ((bf16[16,256,128]{2,1,0:T(8,128)(2,1)}), bf16[16,256,128]{2,1,0:T(8,128)(2,1)S(1)}, u32[]{:S(2)}, u32[]{:S(2)}) async-start(bf16[16,256,128]{2,1,0:T(8,128)(2,1)} %bitcast.61), calls=%async_computation.1 | async-start | bytes 2097152 | tf_op jit(solution)/shard_map/gradient_exchange/all_to_all | solution.py:73
  95.1 3.3 %collective-permute-done.10.refs_0_ = bf16[2,128,1280]{2,1,0:T(8,128)(2,1)S(1)} collective-permute-done((bf16[2,128,1280]{2,1,0:T(8,128)(2,1)S(1)}, bf16[2,128,1280]{2,1,0:T(8,128)(2,1)S(1)}, u32[]{:S(2)}, u32[]{:S(2)}) %collective-permute-start.10) | collective-permute-done | bytes 655392 | tf_op jit(solution)/shard_map/projection/ppermute | solution.py:51
  98.4 11.0 %collective-permute-done.11.refs_1_ = bf16[2,128,1280]{2,1,0:T(8,128)(2,1)} collective-permute-done((bf16[2,128,1280]{2,1,0:T(8,128)(2,1)S(1)}, bf16[2,128,1280]{2,1,0:T(8,128)(2,1)}, u32[]{:S(2)}, u32[]{:S(2)}) %collective-permute-start.11) | collective-permute-done | bytes 655392 | tf_op jit(solution)/shard_map/projection/ppermute | solution.py:51
  109.5 1.9 %all-to-all-done.1 = bf16[16,256,128]{2,1,0:T(8,128)(2,1)S(1)} async-done(((bf16[16,256,128]{2,1,0:T(8,128)(2,1)}), bf16[16,256,128]{2,1,0:T(8,128)(2,1)S(1)}, u32[]{:S(2)}, u32[]{:S(2)}) %all-to-all-start.1) | async-done | bytes 1048608 | tf_op jit(solution)/shard_map/gradient_exchange/all_to_all | solution.py:73
  111.4 1.8 %convolution_bitcast_fusion.2 = f32[256,1280]{1,0:T(8,128)S(1)} fusion(bf16[4,128,1280]{2,1,0:T(8,128)(2,1)} %collective-permute-done.9, bf16[4,4,256,128]{3,2,1,0:T(8,128)(2,1)S(1)} %bitcast.51, s32[]{:T(128)S(6)} %select_n.35), kind=kOutput, calls=%fused_computation.4 | convolution fusion | flops 335544320 | bytes 2883588 | tf_op jit(solution)/shard_map/projection/bcr,brf->cf/dot_general | solution.py:290
  113.2 1.9 %fusion.2 = f32[256,1280]{1,0:T(8,128)S(1)} fusion(f32[256,1280]{1,0:T(8,128)S(1)} %convolution_bitcast_fusion.2, bf16[4,128,1280]{2,1,0:T(8,128)(2,1)} %all-to-all-done, bf16[4,4,256,128]{3,2,1,0:T(8,128)(2,1)S(1)} %bitcast.52, s32[]{:T(128)S(6)} %select_n.33), kind=kOutput, calls=%fused_computation.6 | convolution fusion | flops 335872000 | bytes 4194308 | tf_op jit(solution)/shard_map/projection/bcr,brf->cf/dot_general | solution.py:290
  115.1 1.6 convolution_bitcast_fusion
  116.7 1.8 %fusion.3 = bf16[256,1280]{1,0:T(8,128)(2,1)S(1)} fusion(f32[256,1280]{1,0:T(8,128)S(1)} %convolution_bitcast_fusion, f32[256,1280]{1,0:T(8,128)S(1)} %fusion.2, bf16[4,128,1280]{2,1,0:T(8,128)(2,1)} %collective-permute-done.8, bf16[4,4,256,128]{3,2,1,0:T(8,128)(2,1)S(1)} %bitcast.54, s32[]{:T(128)S(6)} %select_n.37), kind=kOutput, calls=%fused_computation.7 | convolution fusion | flops 336527360 | bytes 4849668 | tf_op jit(solution)/shard_map/projection/bcr,brf->cf/dot_general | solution.py:290
  118.6 6.9 %all_to_all.30 = bf16[2,128,1280]{2,1,0:T(8,128)(2,1)S(1)} all-to-all(bf16[2,128,1280]{2,1,0:T(8,128)(2,1)S(1)} %bitcast.55), channel_id=1, replica_groups=mesh['x'=4,'za'=2,'zb'=4,'y'=4,'zh'=2,'c'=2] {'c'}, dimensions={0} | all-to-all | bytes 1310720 | tf_op jit(solution)/shard_map/core_sum/all_to_all | solution.py:73
  125.5 0.1 reduce_sum.36
  125.6 0.2 copy.18
  125.9 12.1 %all_to_all.31 = bf16[4,2,160,128]{3,2,1,0:T(8,128)(2,1)S(1)} all-to-all(bf16[4,2,160,128]{3,2,1,0:T(8,128)(2,1)S(1)} %copy.19), channel_id=1, replica_groups=mesh['x'=4,'za'=2,'zb'=4,'y'=4,'zh'=2,'c'=2] {'zb'}, dimensions={0} | all-to-all | bytes 655360 | tf_op jit(solution)/shard_map/z_sum/all_to_all | solution.py:73
  138.0 27.3 %all_to_all.32 = bf16[4,160,128]{2,1,0:T(8,128)(2,1)S(1)} all-to-all(bf16[4,160,128]{2,1,0:T(8,128)(2,1)S(1)} %bitcast.62), channel_id=1, replica_groups=mesh['x'=4,'za'=2,'zb'=4,'y'=4,'zh'=2,'c'=2] {'zh','za'}, dimensions={0} | all-to-all | bytes 327680 | tf_op jit(solution)/shard_map/z_sum/all_to_all | solution.py:73
  165.5 13.7 %all_to_all.33 = bf16[8,160,128]{2,1,0:T(8,128)(2,1)S(1)} all-to-all(bf16[8,160,128]{2,1,0:T(8,128)(2,1)S(1)} %broadcast_in_dim.5), channel_id=1, replica_groups=mesh['x'=4,'za'=2,'zb'=4,'y'=4,'zh'=2,'c'=2] {'y','c'}, dimensions={0} | all-to-all | bytes 655360 | tf_op jit(solution)/shard_map/replicate/all_to_all | solution.py:73
  179.3 0.2 copy.21
  179.5 0.2 copy.20
  179.7 0.9 copy_bitcast_fusion
  (36 shorter events, 0.3 us)
Async XLA Ops:
  3.1 49.5 %copy-start = (bf16[1,128,512]{2,1,0:T(8,128)(2,1)S(1)}, bf16[1,128,512]{2,1,0:T(8,128)(2,1)}, u32[]{:S(2)}) copy-start(bf16[1,128,512]{2,1,0:T(8,128)(2,1)} %k_ref.3) | copy-start | bytes 393220
  3.1 49.5 %copy-start.1 = (bf16[1,128,512]{2,1,0:T(8,128)(2,1)S(1)}, bf16[1,128,512]{2,1,0:T(8,128)(2,1)}, u32[]{:S(2)}) copy-start(bf16[1,128,512]{2,1,0:T(8,128)(2,1)} %v_ref.3) | copy-start | bytes 393220
  3.1 49.5 %copy-start.2 = (s32[2]{0:T(128)S(1)}, s32[2]{0:T(128)}, u32[]{:S(2)}) copy-start(s32[2]{0:T(128)} %span_ref.3) | copy-start | bytes 28
  3.1 49.5 %copy-start.3 = (bf16[1,128,2560]{2,1,0:T(8,128)(2,1)S(1)}, bf16[1,128,2560]{2,1,0:T(8,128)(2,1)}, u32[]{:S(2)}) copy-start(bf16[1,128,2560]{2,1,0:T(8,128)(2,1)} %q_ref.1) | copy-start | bytes 1966084
  3.1 49.5 %copy-start.4 = (bf16[1,128,2560]{2,1,0:T(8,128)(2,1)S(1)}, bf16[1,128,2560]{2,1,0:T(8,128)(2,1)}, u32[]{:S(2)}) copy-start(bf16[1,128,2560]{2,1,0:T(8,128)(2,1)} %g_ref.1) | copy-start | bytes 1966084
  3.1 49.5 %copy-start.5 = (s32[1,4096]{1,0:T(1,128)S(1)}, s32[1,4096]{1,0:T(1,128)}, u32[]{:S(2)}) copy-start(s32[1,4096]{1,0:T(1,128)} %seg_ref.1) | copy-start | bytes 49156
  3.1 42.8 %all-to-all-start = ((bf16[4,128,1280]{2,1,0:T(8,128)(2,1)}), bf16[4,128,1280]{2,1,0:T(8,128)(2,1)}, u32[]{:S(2)}, u32[]{:S(2)}) async-start(bf16[4,128,1280]{2,1,0:T(8,128)(2,1)} %feature_blocks.1), calls=%async_computation | async-start | bytes 2621440 | tf_op jit(solution)/shard_map/inputs_exchange/all_to_all | solution.py:73
  9.8 19.7 %collective-permute-start = (bf16[272,512]{1,0:T(8,128)(2,1)}, bf16[272,512]{1,0:T(8,128)(2,1)S(1)}, u32[]{:S(2)}, u32[]{:S(2)}) collective-permute-start(bf16[272,512]{1,0:T(8,128)(2,1)} %packed_tile.1), channel_id=1, source_target_pairs={{496,0},{0,16},{16,32},{32,48},{48,64},{64,80},{80,96},{96,112},{1... | collective-permute-start | bytes 835592 | tf_op jit(solution)/shard_map/keys_values_halo/ppermute | solution.py:31
  13.7 31.0 %collective-permute-start.1 = (bf16[272,512]{1,0:T(8,128)(2,1)}, bf16[272,512]{1,0:T(8,128)(2,1)S(1)}, u32[]{:S(2)}, u32[]{:S(2)}) collective-permute-start(bf16[272,512]{1,0:T(8,128)(2,1)} %packed_tile.1), channel_id=1, source_target_pairs={{480,0},{496,16},{0,32},{16,48},{32,64},{48,80},{64,96},{80,112},{... | collective-permute-start | bytes 835592 | tf_op jit(solution)/shard_map/keys_values_halo/ppermute | solution.py:31
  18.6 34.0 %collective-permute-start.3 = (bf16[272,512]{1,0:T(8,128)(2,1)}, bf16[272,512]{1,0:T(8,128)(2,1)S(1)}, u32[]{:S(2)}, u32[]{:S(2)}) collective-permute-start(bf16[272,512]{1,0:T(8,128)(2,1)} %packed_tile.1), channel_id=1, source_target_pairs={{80,128},{208,256},{336,384},{464,0},{81,129},{209,257},{337,385},... | collective-permute-start | bytes 835592 | tf_op jit(solution)/shard_map/keys_values_halo/ppermute | solution.py:36
  44.6 7.9 %collective-permute-start.2 = (bf16[272,512]{1,0:T(8,128)(2,1)S(1)}, bf16[272,512]{1,0:T(8,128)(2,1)S(1)}, u32[]{:S(2)}, u32[]{:S(2)}) collective-permute-start(bf16[272,512]{1,0:T(8,128)(2,1)S(1)} %collective-permute-done.1.t2_ref), channel_id=1, source_target_pairs={{0,16},{16,32},{32,48},{48,64},{64,80},{80,96},{96,112},{1,17},{17... | collective-permute-start | bytes 835592 | tf_op jit(solution)/shard_map/keys_values_halo/ppermute | solution.py:37
  45.9 33.4 %collective-permute-start.8 = (bf16[4,128,1280]{2,1,0:T(8,128)(2,1)}, bf16[4,128,1280]{2,1,0:T(8,128)(2,1)}, u32[]{:S(2)}, u32[]{:S(2)}) collective-permute-start(bf16[4,128,1280]{2,1,0:T(8,128)(2,1)} %all-to-all-done), channel_id=1, source_target_pairs={{0,4},{4,8},{8,12},{12,0},{1,5},{5,9},{9,13},{13,1},{2,6},{6,10},{... | collective-permute-start | bytes 3932168 | tf_op jit(solution)/shard_map/inputs_exchange/ppermute | solution.py:51
  49.2 33.2 %collective-permute-start.9 = (bf16[4,128,1280]{2,1,0:T(8,128)(2,1)}, bf16[4,128,1280]{2,1,0:T(8,128)(2,1)}, u32[]{:S(2)}, u32[]{:S(2)}) collective-permute-start(bf16[4,128,1280]{2,1,0:T(8,128)(2,1)} %all-to-all-done), channel_id=1, source_target_pairs={{0,12},{4,0},{8,4},{12,8},{1,13},{5,1},{9,5},{13,9},{2,14},{6,2},{... | collective-permute-start | bytes 3932168 | tf_op jit(solution)/shard_map/inputs_exchange/ppermute | solution.py:51
  59.1 8.8 %copy-start.6 = (f32[2,2,128,256]{3,2,1,0:T(8,128)}, f32[2,2,128,256]{3,2,1,0:T(8,128)S(1)}, u32[]{:S(2)}) copy-start(f32[2,2,128,256]{3,2,1,0:T(8,128)S(1)} %get-tuple-element.17.own_ref) | copy-start | bytes 1572868
  59.1 8.7 %collective-permute-start.5 = (bf16[2,2,128,256]{3,2,1,0:T(8,128)(2,1)S(1)}, bf16[2,2,128,256]{3,2,1,0:T(8,128)(2,1)S(1)}, u32[]{:S(2)}, u32[]{:S(2)}) collective-permute-start(bf16[2,2,128,256]{3,2,1,0:T(8,128)(2,1)S(1)} %get-tuple-element.20), channel_id=1, source_target_pairs={{16,0},{32,16},{48,32},{64,48},{80,64},{96,80},{112,96},{17,1},{33... | collective-permute-start | bytes 786440 | tf_op jit(solution)/shard_map/gradient_return/ppermute | solution.py:43
  60.4 27.8 %collective-permute-start.7 = (bf16[2,2,128,256]{3,2,1,0:T(8,128)(2,1)S(1)}, bf16[2,2,128,256]{3,2,1,0:T(8,128)(2,1)S(1)}, u32[]{:S(2)}, u32[]{:S(2)}) collective-permute-start(bf16[2,2,128,256]{3,2,1,0:T(8,128)(2,1)S(1)} %get-tuple-element.20), channel_id=1, source_target_pairs={{0,464},{128,80},{256,208},{384,336},{1,465},{129,81},{257,209},{3... | collective-permute-start | bytes 786440 | tf_op jit(solution)/shard_map/gradient_return/ppermute | solution.py:44
  63.2 24.9 %collective-permute-start.4 = (bf16[2,2,128,256]{3,2,1,0:T(8,128)(2,1)S(1)}, bf16[2,2,128,256]{3,2,1,0:T(8,128)(2,1)S(1)}, u32[]{:S(2)}, u32[]{:S(2)}) collective-permute-start(bf16[2,2,128,256]{3,2,1,0:T(8,128)(2,1)S(1)} %get-tuple-element.18), channel_id=1, source_target_pairs={{16,0},{32,16},{48,32},{64,48},{80,64},{96,80},{112,96},{128,112},... | collective-permute-start | bytes 786440 | tf_op jit(solution)/shard_map/gradient_return/ppermute | solution.py:31
  67.9 20.3 %collective-permute-start.6 = (bf16[2,2,128,256]{3,2,1,0:T(8,128)(2,1)S(1)}, bf16[2,2,128,256]{3,2,1,0:T(8,128)(2,1)S(1)}, u32[]{:S(2)}, u32[]{:S(2)}) collective-permute-start(bf16[2,2,128,256]{3,2,1,0:T(8,128)(2,1)S(1)} %add_convert_fusion), channel_id=1, source_target_pairs={{32,0},{48,16},{64,32},{80,48},{96,64},{112,80},{128,96},{144,112}... | collective-permute-start | bytes 786440 | tf_op jit(solution)/shard_map/gradient_return/ppermute | solution.py:31
  80.4 7.7 %copy-start.7 = (bf16[2,128,1280]{2,1,0:T(8,128)(2,1)}, bf16[2,128,1280]{2,1,0:T(8,128)(2,1)S(1)}, u32[]{:S(2)}) copy-start(bf16[2,128,1280]{2,1,0:T(8,128)(2,1)S(1)} %slice.18.refs_0_) | copy-start | bytes 1966084
  80.4 18.0 %collective-permute-start.10 = (bf16[2,128,1280]{2,1,0:T(8,128)(2,1)S(1)}, bf16[2,128,1280]{2,1,0:T(8,128)(2,1)S(1)}, u32[]{:S(2)}, u32[]{:S(2)}) collective-permute-start(bf16[2,128,1280]{2,1,0:T(8,128)(2,1)S(1)} %slice.18.refs_0_), channel_id=1, source_target_pairs={{0,4},{4,8},{8,12},{12,0},{1,5},{5,9},{9,13},{13,1},{2,6},{6,10},{... | collective-permute-start | bytes 1966088 | tf_op jit(solution)/shard_map/projection/ppermute | solution.py:51
  83.5 4.7 %copy-start.8 = (bf16[2,128,1280]{2,1,0:T(8,128)(2,1)}, bf16[2,128,1280]{2,1,0:T(8,128)(2,1)S(1)}, u32[]{:S(2)}) copy-start(bf16[2,128,1280]{2,1,0:T(8,128)(2,1)S(1)} %slice.19.refs_1_) | copy-start | bytes 1966084
  83.5 26.0 %collective-permute-start.11 = (bf16[2,128,1280]{2,1,0:T(8,128)(2,1)S(1)}, bf16[2,128,1280]{2,1,0:T(8,128)(2,1)}, u32[]{:S(2)}, u32[]{:S(2)}) collective-permute-start(bf16[2,128,1280]{2,1,0:T(8,128)(2,1)S(1)} %slice.19.refs_1_), channel_id=1, source_target_pairs={{0,12},{4,0},{8,4},{12,8},{1,13},{5,1},{9,5},{13,9},{2,14},{6,2},{... | collective-permute-start | bytes 1966088 | tf_op jit(solution)/shard_map/projection/ppermute | solution.py:51
  88.1 0.7 copy-start.12
  88.1 0.8 copy-start.11
  88.2 0.8 copy-start.13
  91.4 19.9 %all-to-all-start.1 = ((bf16[16,256,128]{2,1,0:T(8,128)(2,1)}), bf16[16,256,128]{2,1,0:T(8,128)(2,1)S(1)}, u32[]{:S(2)}, u32[]{:S(2)}) async-start(bf16[16,256,128]{2,1,0:T(8,128)(2,1)} %bitcast.61), calls=%async_computation.1 | async-start | bytes 2097152 | tf_op jit(solution)/shard_map/gradient_exchange/all_to_all | solution.py:73
  98.4 11.0 %copy-start.9 = (bf16[2,128,1280]{2,1,0:T(8,128)(2,1)}, bf16[2,128,1280]{2,1,0:T(8,128)(2,1)S(1)}, u32[]{:S(2)}) copy-start(bf16[2,128,1280]{2,1,0:T(8,128)(2,1)S(1)} %collective-permute-done.10.refs_0_) | copy-start | bytes 1966084
  113.2 1.9 %copy-start.10 = (bf16[2,128,1280]{2,1,0:T(8,128)(2,1)S(1)}, bf16[2,128,1280]{2,1,0:T(8,128)(2,1)}, u32[]{:S(2)}) copy-start(bf16[2,128,1280]{2,1,0:T(8,128)(2,1)} %get-tuple-element.25) | copy-start | bytes 1966084
